TPU v7x, 256 devices: a whole 4x4x8 slice. The times are simulated.
256 devices in a mesh: shape: 4 (over y), space: 64 (over x, z, core).
Axes of the slice: x: 4, y: 4, z: 8, core: 2. Of those that a mesh axis runs over, the one named last changes fastest.
Arguments:
- features: bfloat16 [4, 128, 512, 128], P('shape', 'space'), may hold values from -45 to 45
- gain_one: float32 [128], replicated, may hold values from 0.1 to 1.9
- weight_one: bfloat16 [7, 128, 128], replicated, may hold values from -0.1875 to 0.1875
- gain_two: float32 [128], replicated, may hold values from 0.1 to 1.9
- weight_two: bfloat16 [7, 128, 128], replicated, may hold values from -0.1875 to 0.1875
- live: int32 [4, 128], P('shape', 'space'), may hold values from 0 to 1, as said below
- send_index: int32 [4, 64, 64, 1], P('shape', 'space'), may hold values from -1 to 11, as said below
- recv_index: int32 [4, 128, 6], P('shape', 'space'), may hold values from -1 to 63, as said below
- cotangent: bfloat16 [4, 128, 512, 128], P('shape', 'space'), may hold values from -6 to 6
Outputs:
- output: bfloat16 [4, 128, 512, 128], P('shape', 'space')
- grad_features: bfloat16 [4, 128, 512, 128], P('shape', 'space')
- grad_weight_one: float32 [7, 128, 128], replicated
- grad_weight_two: float32 [7, 128, 128], replicated
- grad_gain_one: float32 [128], replicated
- grad_gain_two: float32 [128], replicated
Inputs may be any that keep to these rules, and one draw needn't show every extreme that they name: The live slots of each device are its first ones, at least 1 of them; in every shape one device has both slots live and another only 1. `recv_index`: -1 where the face has no neighbour slab, always so on slots that are not live; else a position r of the device's receive buffer of 64 slabs, r being the sending device (one slab per sender). No two faces of one device share a position; on every device the slot from some sender is in use; slot 0 of every device has all six faces. send_index[s, d, e, c] is -1 where slot c from device d to device e is unused, else 6 b + f for a live slot b of device d, f being the opposite of the face of the brick of e that reads that slot; it agrees with recv_index.
All inputs are finite; a program needn't handle non-finite values.
Results may differ from a plain program's by a relative error of at most 0.014.
Values may be sent and summed in bfloat16 or wider, within the bound.
A program may use at most 64 MiB of HBM per device.

v0:
```python
import math

import jax
import jax.numpy as jnp
from jax import lax
from jax.sharding import PartitionSpec as P

EDGE = 8


OFFSETS = ((0, 0, 0), (-1, 0, 0), (1, 0, 0), (0, -1, 0), (0, 1, 0), (0, 0, -1), (0, 0, 1))
norm_epsilon = 1e-05


def pre_act(values, gain):
    row_mean = jnp.mean(values, axis=-1, keepdims=True)
    centered = values - row_mean
    variance = jnp.mean(centered * centered, axis=-1, keepdims=True)
    return jax.nn.silu(centered * lax.rsqrt(variance + norm_epsilon) * gain)


def pre_back(brick_cube, gain, upstream):
    outputs, pullback = jax.vjp(pre_act, brick_cube.astype(jnp.float32), gain)
    return pullback(upstream)


def face_slabs(brick_cube):
    brick_count = brick_cube.shape[0]
    edge_len = brick_cube.shape[1]
    last_layer = edge_len - 1
    face_list = [
        brick_cube[:, 0],
        brick_cube[:, last_layer],
        brick_cube[:, :, 0],
        brick_cube[:, :, last_layer],
        brick_cube[:, :, :, 0],
        brick_cube[:, :, :, last_layer],
    ]
    return jnp.stack(
        [
            face_part.reshape(brick_count, edge_len * edge_len, brick_cube.shape[-1])
            for face_part in face_list
        ],
        axis=1,
    )


def pad_cube(brick_cube, halo_slabs):
    brick_count = brick_cube.shape[0]
    edge_len = brick_cube.shape[1]
    channels = brick_cube.shape[-1]
    slab_grid = halo_slabs.reshape(brick_count, 6, edge_len, edge_len, channels)
    far_side = edge_len + 1
    inside = slice(1, far_side)
    padded = jnp.pad(brick_cube, ((0, 0), (1, 1), (1, 1), (1, 1), (0, 0)))
    padded = padded.at[:, 0, inside, inside].set(slab_grid[:, 0])
    padded = padded.at[:, far_side, inside, inside].set(slab_grid[:, 1])
    padded = padded.at[:, inside, 0, inside].set(slab_grid[:, 2])
    padded = padded.at[:, inside, far_side, inside].set(slab_grid[:, 3])
    padded = padded.at[:, inside, inside, 0].set(slab_grid[:, 4])
    padded = padded.at[:, inside, inside, far_side].set(slab_grid[:, 5])
    return padded


def add_faces(volume, face_terms):
    brick_count = volume.shape[0]
    edge_len = volume.shape[1]
    channels = volume.shape[-1]
    term_grid = face_terms.reshape(brick_count, 6, edge_len, edge_len, channels)
    last_layer = edge_len - 1
    volume = volume.at[:, 0].add(term_grid[:, 0])
    volume = volume.at[:, last_layer].add(term_grid[:, 1])
    volume = volume.at[:, :, 0].add(term_grid[:, 2])
    volume = volume.at[:, :, last_layer].add(term_grid[:, 3])
    volume = volume.at[:, :, :, 0].add(term_grid[:, 4])
    volume = volume.at[:, :, :, last_layer].add(term_grid[:, 5])
    return volume


def shifted(padded, tap_index):
    step_i, step_j, step_k = OFFSETS[tap_index]
    edge_len = padded.shape[1] - 2
    window = padded[
        :,
        1 + step_i : 1 + step_i + edge_len,
        1 + step_j : 1 + step_j + edge_len,
        1 + step_k : 1 + step_k + edge_len,
    ]
    return window.reshape(-1, padded.shape[-1])


def convolve(padded, weight):
    running = jnp.dot(shifted(padded, 0), weight[0], preferred_element_type=jnp.float32)
    for tap_index in range(1, len(OFFSETS)):
        running = running + jnp.dot(
            shifted(padded, tap_index), weight[tap_index], preferred_element_type=jnp.float32
        )
    return running


def conv_back(padded, grad_rows, weight):
    brick_count = padded.shape[0]
    edge_len = padded.shape[1] - 2
    channels = padded.shape[-1]
    weight_grad = jnp.stack(
        [
            lax.dot_general(
                shifted(padded, tap_index),
                grad_rows,
                (((0,), (0,)), ((), ())),
                preferred_element_type=jnp.float32,
            )
            for tap_index in range(len(OFFSETS))
        ]
    )
    spread = jnp.zeros(padded.shape, jnp.float32)
    for tap_index in range(len(OFFSETS)):
        step_i, step_j, step_k = OFFSETS[tap_index]
        tap_term = lax.dot_general(
            grad_rows,
            weight[tap_index],
            (((1,), (1,)), ((), ())),
            preferred_element_type=jnp.float32,
        )
        tap_term = tap_term.reshape(brick_count, edge_len, edge_len, edge_len, channels)
        spread = spread.at[
            :,
            1 + step_i : 1 + step_i + edge_len,
            1 + step_j : 1 + step_j + edge_len,
            1 + step_k : 1 + step_k + edge_len,
        ].add(tap_term)
    far_side = edge_len + 1
    inside = slice(1, far_side)
    interior = spread[:, inside, inside, inside]
    face_list = [
        spread[:, 0, inside, inside],
        spread[:, far_side, inside, inside],
        spread[:, inside, 0, inside],
        spread[:, inside, far_side, inside],
        spread[:, inside, inside, 0],
        spread[:, inside, inside, far_side],
    ]
    halo_grad = jnp.stack(
        [face_part.reshape(brick_count, edge_len * edge_len, channels) for face_part in face_list],
        axis=1,
    ).astype(jnp.bfloat16)
    return (weight_grad, interior, halo_grad)


def trade_faces(brick_cube, send_pick, recv_pick, peer_count, slot_count):
    face_rows = face_slabs(brick_cube)
    flat_rows = face_rows.reshape(send_pick.shape[1], -1)
    outgoing = jnp.dot(send_pick, flat_rows, preferred_element_type=jnp.float32).astype(
        jnp.bfloat16
    )
    incoming = lax.all_to_all(
        outgoing.reshape(peer_count, slot_count, -1),
        "space",
        split_axis=0,
        concat_axis=0,
        tiled=True,
    )
    halo_slabs = jnp.dot(
        recv_pick, incoming.reshape(peer_count * slot_count, -1), preferred_element_type=jnp.float32
    ).astype(jnp.bfloat16)
    return halo_slabs.reshape(face_rows.shape)


def return_slabs(halo_grad, send_pick, recv_pick, peer_count, slot_count):
    flat_rows = halo_grad.reshape(recv_pick.shape[0], -1)
    outgoing = lax.dot_general(
        recv_pick, flat_rows, (((0,), (0,)), ((), ())), preferred_element_type=jnp.float32
    ).astype(jnp.bfloat16)
    incoming = lax.all_to_all(
        outgoing.reshape(peer_count, slot_count, -1),
        "space",
        split_axis=0,
        concat_axis=0,
        tiled=True,
    )
    summed = lax.dot_general(
        send_pick,
        incoming.reshape(peer_count * slot_count, -1),
        (((0,), (0,)), ((), ())),
        preferred_element_type=jnp.float32,
    )
    return summed.reshape(halo_grad.shape)


def forward_conv(brick_cube, weight, send_pick, recv_pick, peer_count, slot_count):
    halo_slabs = trade_faces(brick_cube, send_pick, recv_pick, peer_count, slot_count)
    padded = pad_cube(brick_cube, halo_slabs)
    result = convolve(padded, weight).reshape(brick_cube.shape)
    return (result, padded)


def shards(
    features, gain_one, weight_one, gain_two, weight_two, live, send_index, recv_index, cotangent
):
    brick_count = features.shape[1]
    channels = features.shape[3]
    edge_len = EDGE
    peer_count = lax.axis_size("space")
    slot_count = send_index.shape[3]
    cube_shape = (brick_count, edge_len, edge_len, edge_len, channels)
    cubes_in = features.reshape(cube_shape)
    cot_cube = cotangent.reshape(cube_shape)
    alive_rows = (live.reshape(brick_count) > 0)[:, None, None, None, None]
    send_codes = send_index.reshape(peer_count * slot_count)
    places = recv_index.reshape(brick_count * 6)
    send_pick = (
        send_codes[:, None] == jnp.arange(brick_count * 6, dtype=jnp.int32)[None, :]
    ).astype(jnp.bfloat16)
    recv_pick = (
        places[:, None] == jnp.arange(peer_count * slot_count, dtype=jnp.int32)[None, :]
    ).astype(jnp.bfloat16)
    acts_one = pre_act(cubes_in.astype(jnp.float32), gain_one).astype(jnp.bfloat16)
    conv_one, padded_one = forward_conv(
        acts_one, weight_one, send_pick, recv_pick, peer_count, slot_count
    )
    hidden = conv_one.astype(jnp.bfloat16)
    acts_two = pre_act(hidden.astype(jnp.float32), gain_two).astype(jnp.bfloat16)
    conv_two, padded_two = forward_conv(
        acts_two, weight_two, send_pick, recv_pick, peer_count, slot_count
    )
    output = jnp.where(
        alive_rows, cubes_in.astype(jnp.float32) + conv_two, jnp.zeros(conv_two.shape, jnp.float32)
    ).astype(jnp.bfloat16)
    grad_rows = jnp.where(alive_rows, cot_cube, jnp.zeros_like(cot_cube))
    weight_grad_two, interior_two, halo_grad_two = conv_back(
        padded_two, grad_rows.reshape(-1, channels), weight_two
    )
    returned_two = return_slabs(halo_grad_two, send_pick, recv_pick, peer_count, slot_count)
    grad_hidden, gain_grad_two = pre_back(hidden, gain_two, add_faces(interior_two, returned_two))
    grad_hidden = grad_hidden.astype(jnp.bfloat16)
    weight_grad_one, interior_one, halo_grad_one = conv_back(
        padded_one, grad_hidden.reshape(-1, channels), weight_one
    )
    returned_one = return_slabs(halo_grad_one, send_pick, recv_pick, peer_count, slot_count)
    grad_input, gain_grad_one = pre_back(cubes_in, gain_one, add_faces(interior_one, returned_one))
    direct = jnp.where(
        alive_rows, cot_cube.astype(jnp.float32), jnp.zeros(grad_input.shape, jnp.float32)
    )
    grad_features = (direct + grad_input).astype(jnp.bfloat16)
    weight_sum_one, weight_sum_two, gain_sum_one, gain_sum_two = lax.psum(
        (weight_grad_one, weight_grad_two, gain_grad_one, gain_grad_two), ("shape", "space")
    )
    total_rows = (
        features.shape[0] * lax.axis_size("shape") * brick_count * peer_count * features.shape[2]
    )
    grad_scale = 1.0 / math.sqrt(total_rows)
    return (
        output.reshape(features.shape),
        grad_features.reshape(features.shape),
        weight_sum_one * grad_scale,
        weight_sum_two * grad_scale,
        gain_sum_one * grad_scale,
        gain_sum_two * grad_scale,
    )


def solution(mesh):
    in_specs = (
        P("shape", "space", None, None),
        P(),
        P(),
        P(),
        P(),
        P("shape", "space"),
        P("shape", "space", None, None),
        P("shape", "space", None),
        P("shape", "space", None, None),
    )
    out_specs = (
        P("shape", "space", None, None),
        P("shape", "space", None, None),
        P(),
        P(),
        P(),
        P(),
    )
    return jax.shard_map(shards, mesh=mesh, in_specs=in_specs, out_specs=out_specs, check_vma=False)
```

profile of v0, /device:TPU:1, one launch (start us, length us, event | category | flops | bytes accessed | tf_op | source)
XLA Modules:
  0.0 569.1 jit_solution(17979509776324319021)
XLA Ops:
  16.4 13.3 %all-to-all-start = ((bf16[64,2,4096]{2,1,0:T(2,128)(2,1)}), bf16[64,2,4096]{2,1,0:T(2,128)(2,1)}, u32[]{:S(2)}, u32[]{:S(2)}) async-start(bf16[64,2,4096]{2,1,0:T(2,128)(2,1)} %reshape.1985), calls=%async_computation | async-start | bytes 2097152 | tf_op jit(solution)/shard_map/all_to_all | solution.py:156
  32.2 2.7 scatter-add.89
  35.2 2.7 scatter-add.90
  38.1 2.7 scatter-add.91
  41.0 2.7 scatter-add.94
  44.2 2.7 scatter-add.96
  55.1 3.3 reduce.80
  58.5 2.6 reshape.1989
  61.1 10.9 %all-to-all-start.2 = ((bf16[64,2,4096]{2,1,0:T(2,128)(2,1)}), bf16[64,2,4096]{2,1,0:T(2,128)(2,1)}, u32[]{:S(2)}, u32[]{:S(2)}) async-start(bf16[64,2,4096]{2,1,0:T(2,128)(2,1)} %reshape.1989), calls=%async_computation.2 | async-start | bytes 2097152 | tf_op jit(solution)/shard_map/all_to_all | solution.py:174
  72.0 7.5 %reshape.1986 = bf16[64,1,8192]{2,1,0:T(2,128)(2,1)} reshape(bf16[64,2,4096]{2,1,0:T(2,128)(2,1)} %all-to-all-done) | data formatting | bytes 2097152
  79.5 2.8 convolution_convert_fusion.5
  89.5 10.8 %all-to-all-done.2 = bf16[64,2,4096]{2,1,0:T(2,128)(2,1)} async-done(((bf16[64,2,4096]{2,1,0:T(2,128)(2,1)}), bf16[64,2,4096]{2,1,0:T(2,128)(2,1)}, u32[]{:S(2)}, u32[]{:S(2)}) %all-to-all-start.2) | async-done | bytes 1048608 | tf_op jit(solution)/shard_map/all_to_all | solution.py:174
  100.3 7.5 %reshape.1990 = bf16[64,1,8192]{2,1,0:T(2,128)(2,1)} reshape(bf16[64,2,4096]{2,1,0:T(2,128)(2,1)} %all-to-all-done.2) | data formatting | bytes 2097152
  107.8 2.7 copy.213
  118.1 2.7 scatter-add.110
  121.1 2.9 scatter-add.111
  124.2 2.7 scatter-add.114
  127.1 2.7 scatter-add.115
  130.3 2.7 scatter-add.119
  137.7 2.6 reshape.1991
  140.3 6.4 %all-to-all-start.3 = ((bf16[64,2,4096]{2,1,0:T(2,128)(2,1)}), bf16[64,2,4096]{2,1,0:T(2,128)(2,1)}, u32[]{:S(2)}, u32[]{:S(2)}) async-start(bf16[64,2,4096]{2,1,0:T(2,128)(2,1)} %reshape.1991), calls=%async_computation.3 | async-start | bytes 2097152 | tf_op jit(solution)/shard_map/all_to_all | solution.py:174
  152.7 3.3 reduce.82
  156.0 2.6 reshape.1987
  165.3 9.9 %all-to-all-done.3 = bf16[64,2,4096]{2,1,0:T(2,128)(2,1)} async-done(((bf16[64,2,4096]{2,1,0:T(2,128)(2,1)}), bf16[64,2,4096]{2,1,0:T(2,128)(2,1)}, u32[]{:S(2)}, u32[]{:S(2)}) %all-to-all-start.3) | async-done | bytes 1048608 | tf_op jit(solution)/shard_map/all_to_all | solution.py:174
  175.1 6.4 %all-to-all-start.1 = ((bf16[64,2,4096]{2,1,0:T(2,128)(2,1)}), bf16[64,2,4096]{2,1,0:T(2,128)(2,1)}, u32[]{:S(2)}, u32[]{:S(2)}) async-start(bf16[64,2,4096]{2,1,0:T(2,128)(2,1)} %reshape.1987), calls=%async_computation.1 | async-start | bytes 2097152 | tf_op jit(solution)/shard_map/all_to_all | solution.py:156
  181.6 2.2 fusion.15
  183.8 7.5 %reshape.1992 = bf16[64,1,8192]{2,1,0:T(2,128)(2,1)} reshape(bf16[64,2,4096]{2,1,0:T(2,128)(2,1)} %all-to-all-done.3) | data formatting | bytes 2097152
  191.3 2.7 copy.212
  198.2 11.8 %all-to-all-done.1 = bf16[64,2,4096]{2,1,0:T(2,128)(2,1)} async-done(((bf16[64,2,4096]{2,1,0:T(2,128)(2,1)}), bf16[64,2,4096]{2,1,0:T(2,128)(2,1)}, u32[]{:S(2)}, u32[]{:S(2)}) %all-to-all-start.1) | async-done | bytes 1048608 | tf_op jit(solution)/shard_map/all_to_all | solution.py:156
  210.0 6.5 %reshape.1988 = bf16[64,1,8192]{2,1,0:T(2,128)(2,1)S(1)} reshape(bf16[64,2,4096]{2,1,0:T(2,128)(2,1)} %all-to-all-done.1) | data formatting | bytes 2097152
  234.8 76.0 %all-reduce.4 = (f32[128]{0:T(128)S(1)}, f32[128]{0:T(128)S(1)}) all-reduce(f32[128]{0:T(128)S(1)} %get-tuple-element.462, f32[128]{0:T(128)S(1)} %get-tuple-element.464), channel_id=1, replica_groups=mesh['shape'=4,'space'=64] {'shape','space'}, use_global_device_ids=true, to_apply=%region_11.12 | all-reduce | flops 256 | bytes 2048 | tf_op jit(solution)/shard_map/psum | solution.py:245
  312.8 246.8 %all-reduce.8.cloned.1.call-done = (f32[7,128,128]{2,1,0:T(8,128)}, f32[7,128,128]{2,1,0:T(8,128)}) async-done(((f32[7,128,128]{2,1,0:T(8,128)}, f32[7,128,128]{2,1,0:T(8,128)}), (f32[7,128,128]{2,1,0:T(8,128)}, f32[7,128,128]{2,1,0:T(8,128)})) %all-reduce.8.cloned.1.call-update) | async-done | bytes 917520 | tf_op jit(solution)/shard_map/psum | solution.py:245
  (244 shorter events, 79.9 us)
Async XLA Ops:
  9.7 2.7 copy-start.4
  9.8 2.3 copy-start.21
  9.8 2.5 copy-start.6
  9.9 2.5 copy-start.26
  16.4 13.5 %copy-start.30 = (s32[1,2]{1,0:T(1,128)S(1)}, s32[1,2]{1,0:T(1,128)}, u32[]{:S(2)}) copy-start(s32[1,2]{1,0:T(1,128)} %param.90) | copy-start | bytes 28
  16.4 13.5 %copy-start.10 = (bf16[1,2,512,128]{3,2,1,0:T(8,128)(2,1)S(1)}, bf16[1,2,512,128]{3,2,1,0:T(8,128)(2,1)}, u32[]{:S(2)}) copy-start(bf16[1,2,512,128]{3,2,1,0:T(8,128)(2,1)} %param.93) | copy-start | bytes 786436
  16.4 44.7 %all-to-all-start = ((bf16[64,2,4096]{2,1,0:T(2,128)(2,1)}), bf16[64,2,4096]{2,1,0:T(2,128)(2,1)}, u32[]{:S(2)}, u32[]{:S(2)}) async-start(bf16[64,2,4096]{2,1,0:T(2,128)(2,1)} %reshape.1985), calls=%async_computation | async-start | bytes 2097152 | tf_op jit(solution)/shard_map/all_to_all | solution.py:156
  32.0 2.9 copy-start.17
  47.6 1.1 copy-start.29
  47.6 5.7 %copy-start.23 = (bf16[2,8,8,1,128]{4,3,2,1,0:T(2,128)(2,1)S(1)}, bf16[2,8,8,1,128]{4,3,2,1,0:T(2,128)(2,1)}, u32[]{:S(2)}) copy-start(bf16[2,8,8,1,128]{4,3,2,1,0:T(2,128)(2,1)} %slice.2143) | copy-start | bytes 98308
  61.1 39.2 %all-to-all-start.2 = ((bf16[64,2,4096]{2,1,0:T(2,128)(2,1)}), bf16[64,2,4096]{2,1,0:T(2,128)(2,1)}, u32[]{:S(2)}, u32[]{:S(2)}) async-start(bf16[64,2,4096]{2,1,0:T(2,128)(2,1)} %reshape.1989), calls=%async_computation.2 | async-start | bytes 2097152 | tf_op jit(solution)/shard_map/all_to_all | solution.py:174
  86.0 1.2 copy-start.15
  89.0 26.0 %copy-start.13 = (f32[2,8,8,8]{3,2,1,0:T(8,128)}, f32[2,8,8,8]{3,2,1,0:T(8,128)S(1)}, u32[]{:S(2)}) copy-start(f32[2,8,8,8]{3,2,1,0:T(8,128)S(1)} %div.59) | copy-start | bytes 12292
  89.5 25.6 %copy-start.14 = (f32[2,8,8,8]{3,2,1,0:T(8,128)}, f32[2,8,8,8]{3,2,1,0:T(8,128)S(1)}, u32[]{:S(2)}) copy-start(f32[2,8,8,8]{3,2,1,0:T(8,128)S(1)} %rsqrt.23) | copy-start | bytes 12292
  110.8 3.8 copy-start.28
  115.6 1.9 copy-start.16
  140.3 34.9 %all-to-all-start.3 = ((bf16[64,2,4096]{2,1,0:T(2,128)(2,1)}), bf16[64,2,4096]{2,1,0:T(2,128)(2,1)}, u32[]{:S(2)}, u32[]{:S(2)}) async-start(bf16[64,2,4096]{2,1,0:T(2,128)(2,1)} %reshape.1991), calls=%async_computation.3 | async-start | bytes 2097152 | tf_op jit(solution)/shard_map/all_to_all | solution.py:174
  146.7 2.1 copy-start.25
  146.7 2.8 copy-start.24
  158.7 2.0 copy-start.1
  175.1 34.9 %all-to-all-start.1 = ((bf16[64,2,4096]{2,1,0:T(2,128)(2,1)}), bf16[64,2,4096]{2,1,0:T(2,128)(2,1)}, u32[]{:S(2)}, u32[]{:S(2)}) async-start(bf16[64,2,4096]{2,1,0:T(2,128)(2,1)} %reshape.1987), calls=%async_computation.1 | async-start | bytes 2097152 | tf_op jit(solution)/shard_map/all_to_all | solution.py:156
  181.5 378.1 %all-reduce.8.cloned.1.call-start = ((), (), s32[]{:S(2)}) async-start(), calls=%async_computation.4 | async-start | bytes 1835008 | tf_op jit(solution)/shard_map/psum | solution.py:245
  221.4 1.3 copy-start.11
  228.2 1.0 copy-start.7
  228.2 1.0 copy-start.27
  229.1 2.9 copy-start.18
  229.2 3.0 copy-start.9
  230.7 1.3 copy-start.19
  230.7 1.7 copy-start.8
  233.3 78.1 %copy-start.12 = (bf16[1,2,512,128]{3,2,1,0:T(8,128)(2,1)S(1)}, bf16[1,2,512,128]{3,2,1,0:T(8,128)(2,1)}, u32[]{:S(2)}) copy-start(bf16[1,2,512,128]{3,2,1,0:T(8,128)(2,1)} %param.93) | copy-start | bytes 786436
  233.3 78.1 %copy-start.20 = (f32[2,8,8,8]{3,2,1,0:T(8,128)S(1)}, f32[2,8,8,8]{3,2,1,0:T(8,128)}, u32[]{:S(2)}) copy-start(f32[2,8,8,8]{3,2,1,0:T(8,128)} %copy-done.19) | copy-start | bytes 12292
  233.3 78.1 %copy-start.22 = (f32[2,8,8,8]{3,2,1,0:T(8,128)S(1)}, f32[2,8,8,8]{3,2,1,0:T(8,128)}, u32[]{:S(2)}) copy-start(f32[2,8,8,8]{3,2,1,0:T(8,128)} %negate_multiply_fusion) | copy-start | bytes 12292
  (4 other events, 4.0 us)
Sparse Core Ops, SparseCore 0:
  311.0 248.5 all-reduce.7
where the time goes:
time: 579 us; the launch traced here: 569 us
  waiting for transfers between devices  279 us (48%)
  local copies, waits for them, and re-layouts  101 us (17%)
  blocking collectives  76 us (13%)
  starting transfers between devices  37 us (6%)
  matrix products  32.7 us (6%)
  other arithmetic  27.2 us (5%)
  between operations  15.8 us (3%)
    psum x1, waiting for transfers between devices, shards(): lax.psum((weight_grad_one, weight_grad_two, gain_grad_one, gain_grad_two)...  247 us
    psum x1, blocking collectives, shards(): lax.psum((weight_grad_one, weight_grad_two, gain_grad_one, gain_grad_two)...  76 us
    unnamed x106, local copies, waits for them, and re-layouts  53.6 us
    scatter-add x12, local copies, waits for them, and re-layouts, conv_back(): spread = spread.at[:, 1 + step_i:1 + step_i + edge_len, 1 + step_j:1 + st...  27.4 us
    all_to_all x2, waiting for transfers between devices, return_slabs(): lax.all_to_all(outgoing.reshape(peer_count, slot_count, -1), 'space', spl...  20.6 us
    all_to_all x2, starting transfers between devices, trade_faces(): lax.all_to_all(outgoing.reshape(peer_count, slot_count, -1), 'space', spl...  19.7 us
    all_to_all x2, starting transfers between devices, return_slabs(): lax.all_to_all(outgoing.reshape(peer_count, slot_count, -1), 'space', spl...  17.3 us
    dot_general x14, matrix products, conv_back(): lax.dot_general(shifted(padded, tap_index), grad_rows, (((0,), (0,)), (()...  15.3 us
  transfers between devices with their start and end apart: 5, of which 4 were waited for; matrix products, arithmetic and copies ran while one was open for 15% of the time, Pallas kernels for 0%

commit v1 on v0

v1 whole, which is shorter than its diff:
```python
import functools
import math

import jax
import jax.numpy as jnp
from jax import lax
from jax.experimental import pallas as pl
from jax.experimental.pallas import tpu as pltpu
from jax.sharding import PartitionSpec as P

MESH = pl.DeviceIdType.MESH
F32 = jnp.float32
BF16 = jnp.bfloat16
EPS = 1e-05
SWAP = (0, 2, 1, 4, 3, 6, 5)
XD, ZD, YD = 4, 8, 4
LO = 8


def norm(v):
    c = v - jnp.mean(v, axis=-1, keepdims=True)
    r = lax.rsqrt(jnp.mean(c * c, axis=-1, keepdims=True) + EPS)
    return c * r, r


def silu_parts(t):
    s = 1.0 / (1.0 + jnp.exp(-t))
    return t * s, s * (1.0 + t * (1.0 - s))


def rounded(v):
    return v.astype(BF16).astype(F32)


def dot(a, b):
    return jnp.dot(a, b, preferred_element_type=F32)


def dot_t(a, b):
    return lax.dot_general(a, b, (((0,), (0,)), ((), ())), preferred_element_type=F32)


def kernel(
    scale,
    send_s,
    recv_s,
    live_s,
    x_ref,
    g1_ref,
    w1_ref,
    g2_ref,
    w2_ref,
    cot_ref,
    out_ref,
    gf_ref,
    gw1_ref,
    gw2_ref,
    gg1_ref,
    gg2_ref,
    *scratch,
):
    gath = [scratch[i * 8 : i * 8 + 8] for i in range(4)]
    inb = scratch[32:36]
    (
    outb,
    tbl,
    a32,
    s32,
    u7,
    v7,
    hid,
    act2,
    acc,
    acc2,
    hal,
    hald,
    ret,
    wt1,
    wt2,
    wg,
    fin,
    ac_out,
    ac_in,
    ay_out,
    ay_in,
    ax_out,
    ax_in,
    az,
    ring_send,
    ring_recv,
    x_send,
    x_recv,
    t_sem,
    ar_sem,
    ag_sem,
    ) = scratch[36:]
    y = lax.axis_index("shape")
    sp = lax.axis_index("space")
    xi = sp // 16
    zi = (sp // 2) % ZD
    ci = sp % 2

    def dev(yy, xx, zz, cc):
        return (yy, (xx * ZD + zz) * 2 + cc)

    def z_dev(o):
        return dev(y, xi, (zi + o) % ZD, ci)

    def row_dev(l):
        return dev(y, (xi + l // 2) % XD, zi, (ci + l % 2) % 2)

    def x_dev(o):
        return dev(y, (xi + o) % XD, zi, ci)

    def y_dev(o):
        return dev((y + o) % YD, xi, zi, ci)

    sibling = dev(y, xi, zi, 1 - ci)

    barrier = pltpu.get_barrier_semaphore()
    for o in range(1, ZD):
        pl.semaphore_signal(barrier, inc=1, device_id=z_dev(o), device_id_type=MESH)
    for l in range(1, 8):
        pl.semaphore_signal(barrier, inc=1, device_id=row_dev(l), device_id_type=MESH)
    for o in range(1, YD):
        pl.semaphore_signal(barrier, inc=1, device_id=y_dev(o), device_id_type=MESH)

    def push(src, dst, ssem, rsem, target):
        pltpu.make_async_remote_copy(
            src_ref=src,
            dst_ref=dst,
            send_sem=ssem,
            recv_sem=rsem,
            device_id=target,
            device_id_type=MESH,
        ).start()

    def wait(ref, sem):
        pltpu.make_async_copy(ref, ref, sem).wait()

    def ring(pay, src, dst, b, step):
        push(
            gath[pay][src].at[pl.ds(b * 6, 6)],
            gath[pay][dst].at[pl.ds(b * 6, 6)],
            ring_send.at[pay, dst, b],
            ring_recv.at[pay, dst, b],
            z_dev(step),
        )

    def ring_wait(pay, slot, b):
        wait(gath[pay][slot].at[pl.ds(b * 6, 6)], ring_recv.at[pay, slot, b])

    def forward(pay, h):
        if h == 0:
            for b in range(2):
                ring(pay, 0, 1, b, 1)
                ring(pay, 0, ZD - 1, b, ZD - 1)
        elif h < 4:
            for b in range(2):
                ring_wait(pay, h, b)
                if h < 3 or b == 0:
                    ring(pay, h, h + 1, b, 1)
            for b in range(2):
                ring_wait(pay, ZD - h, b)
                if h < 3 or b == 1:
                    ring(pay, ZD - h, ZD - 1 - h, b, ZD - 1)
        else:
            ring_wait(pay, 4, 0)
            ring_wait(pay, 4, 1)

    def select(pay, o):
        row = tbl[o, pl.ds(o, 1), :]
        for l in range(8):
            lane = l + 8 * (pay % 2)
            code = jnp.maximum(row[0, lane], 0)
            slab = gath[pay][o][code]
            if l == 0:
                inb[pay][o * 8] = slab
            else:
                outb[pay, o, l] = slab
                push(
                    outb.at[pay, o, l],
                    inb[pay].at[o * 8 + l],
                    x_send.at[pay, o],
                    x_recv.at[pay, o],
                    row_dev(l),
                )

    def arrived(pay, o):
        wait(inb[pay].at[pl.ds(o * 8 + 1, 7)], x_recv.at[pay, o])

    def hop(pay, h):
        forward(pay, h)
        select(pay, h)
        if 0 < h < 4:
            select(pay, ZD - h)

    def add_returns(pay, o, first):
        codes = []
        for l in range(8):
            r = ((xi - l // 2 + XD) % XD * ZD + (zi - o + ZD) % ZD) * 2 + (ci + l % 2) % 2
            codes.append(send_s[r])

        def one(q, carry):
            total = jnp.zeros((64, 128), F32) if first else ret[q]
            for l in range(8):
                m = (codes[l] == q).astype(F32)
                total = total + inb[pay][o * 8 + l].astype(F32) * m
            ret[q] = total
            return carry

        lax.fori_loop(0, 12, one, 0)

    def take_halo(pay, q):
        r = recv_s[q]
        p = jnp.maximum(r, 0)
        idx = ((zi - (p // 2) % ZD + ZD) % ZD) * 8 + ((xi - p // 16 + XD) % XD) * 2 + (ci + p % 2) % 2
        return inb[pay][idx].astype(F32) * (r >= 0).astype(F32)

    def chunks(n, size, body):
        def step(i, carry):
            body(pl.multiple_of(i * size, size))
            return carry

        lax.fori_loop(0, n, step, 0)

    def faces(pay):
        for n in range(2):
            base = LO + n * 512
            cube = a32[pl.ds(base, 512), :].reshape(8, 8, 8, 128)
            gath[pay][0][n * 6] = a32[pl.ds(base, 64), :].astype(BF16)
            gath[pay][0][n * 6 + 1] = a32[pl.ds(base + 448, 64), :].astype(BF16)
            gath[pay][0][n * 6 + 2] = cube[:, 0].reshape(64, 128).astype(BF16)
            gath[pay][0][n * 6 + 3] = cube[:, 7].reshape(64, 128).astype(BF16)
            gath[pay][0][n * 6 + 4] = a32[pl.ds(base, 64, stride=8), :].astype(BF16)
            gath[pay][0][n * 6 + 5] = a32[pl.ds(base + 7, 64, stride=8), :].astype(BF16)

    def columns(dst, halo):
        for n in range(2):
            base = LO + n * 512
            rows = pl.ds(n * 512, 512)

            def h(f):
                return jnp.zeros((64, 128), F32) if halo is None else halo[n * 6 + f]

            body = a32[pl.ds(base, 512), :]
            half = body.astype(BF16)
            dst[rows, 0:128] = half
            dst[pl.ds(n * 512, 64), 128:256] = h(0).astype(BF16)
            dst[pl.ds(n * 512 + 64, 448), 128:256] = half[:448]
            dst[pl.ds(n * 512, 448), 256:384] = half[64:]
            dst[pl.ds(n * 512 + 448, 64), 256:384] = h(1).astype(BF16)
            cube = body.reshape(8, 8, 8, 128)
            low = jnp.concatenate([h(2).reshape(8, 1, 8, 128), cube[:, :7]], axis=1)
            dst[rows, 384:512] = low.reshape(512, 128).astype(BF16)
            high = jnp.concatenate([cube[:, 1:], h(3).reshape(8, 1, 8, 128)], axis=1)
            dst[rows, 512:640] = high.reshape(512, 128).astype(BF16)
            s32[...] = a32[pl.ds(base - 1, 512), :]
            s32[pl.ds(0, 64, stride=8), :] = h(4)
            dst[rows, 640:768] = s32[...].astype(BF16)
            s32[...] = a32[pl.ds(base + 1, 512), :]
            s32[pl.ds(7, 64, stride=8), :] = h(5)
            dst[rows, 768:896] = s32[...].astype(BF16)

    def add_face(target, n, f, term):
        base = n * 512
        if f == 0:
            target[pl.ds(base, 64), :] += term
        elif f == 1:
            target[pl.ds(base + 448, 64), :] += term
        elif f < 4:
            for i in range(8):
                target[pl.ds(base + i * 64 + (f - 2) * 56, 8), :] += term[i * 8 : i * 8 + 8]
        else:
            rows = pl.ds(base + (f - 4) * 7, 64, stride=8)
            target[rows, :] = target[rows, :] + term

    gain1 = g1_ref[...]
    gain2 = g2_ref[...]
    alive = [live_s[n].astype(F32) for n in range(2)]

    a32[pl.ds(LO, 1024), :] = x_ref[...].astype(F32)
    faces(0)
    step_id = lax.broadcasted_iota(jnp.int32, (8, 128), 0)
    lane_id = lax.broadcasted_iota(jnp.int32, (8, 128), 1)
    in_x = lane_id % 8
    target_id = (
        ((xi + in_x // 2) % XD) * (2 * ZD) + ((zi + step_id) % ZD) * 2 + (ci + in_x % 2) % 2
    )
    codes = jnp.full((8, 128), -1, jnp.int32)
    for e in range(64):
        codes = jnp.where(target_id == e, send_s[e], codes)
    back = jnp.full((8, 128), -1, jnp.int32)
    for q in range(12):
        back = jnp.where(target_id == recv_s[q], q, back)
    tbl[0] = jnp.where(lane_id < 8, codes, back)

    pl.semaphore_wait(barrier, 17)
    for o in range(1, ZD):
        push(tbl.at[0], tbl.at[o], t_sem.at[0], t_sem.at[1], z_dev(o))
    forward(0, 0)

    for n in range(2):
        a32[pl.ds(LO + n * 512, 512), :] = cot_ref[pl.ds(n * 512, 512), :].astype(F32) * alive[n]
    faces(1)
    forward(1, 0)
    select(0, 0)
    select(1, 0)
    for t in range(7):
        src = pl.ds(SWAP[t] * 128, 128)
        wt1[pl.ds(t * 128, 128), :] = w1_ref[src, :].astype(F32).T.astype(BF16)
        wt2[pl.ds(t * 128, 128), :] = w2_ref[src, :].astype(F32).T.astype(BF16)

    wait(tbl.at[pl.ds(1, 7)], t_sem.at[1])
    for h in range(1, 5):
        hop(0, h)
        hop(1, h)
    for o in range(8):
        arrived(0, o)

    def halo_one(q, carry):
        xhat, _ = norm(take_halo(0, q))
        act, slope = silu_parts(xhat * gain1)
        hal[q] = rounded(act)
        hald[q] = slope * xhat
        return carry

    lax.fori_loop(0, 12, halo_one, 0)

    def act_one(r):
        xhat, _ = norm(x_ref[pl.ds(r, 128), :].astype(F32))
        a32[pl.ds(LO + r, 128), :] = rounded(silu_parts(xhat * gain1)[0])

    chunks(8, 128, act_one)
    columns(u7, hal)

    def hidden_rows(r):
        rows = pl.ds(r, 256)
        h = dot(u7[rows, :], w1_ref[...]).astype(BF16)
        hid[rows, :] = h
        xhat, _ = norm(h.astype(F32))
        a = silu_parts(xhat * gain2)[0].astype(BF16)
        act2[rows, :] = a
        a32[pl.ds(LO + r, 256), :] = a.astype(F32)

    chunks(4, 256, hidden_rows)
    faces(2)
    forward(2, 0)
    select(2, 0)

    for o in range(8):
        arrived(1, o)
        add_returns(1, o, o == 0)
    for n in range(2):
        a32[pl.ds(LO + n * 512, 512), :] = cot_ref[pl.ds(n * 512, 512), :].astype(F32) * alive[n]
    columns(v7, ret)

    wg[pl.ds(1792, 256), :] = jnp.zeros((256, 128), F32)

    def pre_back(v, gain, upstream):
        xhat, r = norm(v)
        _, slope = silu_parts(xhat * gain)
        dt = upstream * slope
        d = dt * gain
        mean_d = jnp.mean(d, axis=-1, keepdims=True)
        mean_dx = jnp.mean(d * xhat, axis=-1, keepdims=True)
        return r * (d - mean_d - xhat * mean_dx), dt * xhat

    def grad_hidden_rows(r):
        up = dot(v7[pl.ds(r, 256), :], wt2[...])
        grad, per = pre_back(hid[pl.ds(r, 256), :].astype(F32), gain2, up)
        a32[pl.ds(LO + r, 256), :] = rounded(grad)
        wg[pl.ds(1793, 1), :] += jnp.sum(per, axis=0, keepdims=True)

    chunks(4, 256, grad_hidden_rows)
    faces(3)
    forward(3, 0)
    select(3, 0)

    a2 = act2[...]
    for t in range(7):
        wg[pl.ds(896 + SWAP[t] * 128, 128), :] = dot_t(a2, v7[:, t * 128 : t * 128 + 128])
    gh = a32[pl.ds(LO, 1024), :].astype(BF16)
    for t in range(7):
        wg[pl.ds(t * 128, 128), :] = dot_t(u7[:, t * 128 : t * 128 + 128], gh)

    columns(v7, None)

    def inner_one(r):
        rows = pl.ds(r, 256)
        up = dot(v7[rows, :], wt1[...])
        acc2[rows, :] = up
        xhat, _ = norm(x_ref[rows, :].astype(F32))
        slope = silu_parts(xhat * gain1)[1]
        wg[pl.ds(1792, 1), :] += jnp.sum(up * slope * xhat, axis=0, keepdims=True)

    chunks(4, 256, inner_one)
    for f in range(6):
        w = wt1[pl.ds(SWAP[f + 1] * 128, 128), :]
        for n in range(2):
            q = n * 6 + f
            term = rounded(dot(gath[3][0][q], w)) * hald[q]
            wg[pl.ds(1792, 1), :] += jnp.sum(term, axis=0, keepdims=True)

    mine = pl.multiple_of(ci * 1024, 1024)
    other = pl.multiple_of((1 - ci) * 1024, 1024)
    ac_out[...] = wg[pl.ds(other, 1024), :].astype(BF16)
    push(ac_out, ac_in, ar_sem.at[0, 0], ar_sem.at[0, 1], sibling)

    hop(2, 1)
    hop(3, 1)

    wait(ac_in, ar_sem.at[0, 1])
    wg[pl.ds(mine, 1024), :] += ac_in[...].astype(F32)
    for o in range(1, YD):
        start = pl.multiple_of(mine + ((y + o) % YD) * 256, 256)
        ay_out[o] = wg[pl.ds(start, 256), :].astype(BF16)
        push(ay_out.at[o], ay_in.at[o], ar_sem.at[1, 0], ar_sem.at[1, 1], y_dev(o))

    hop(2, 2)
    hop(3, 2)

    a32[pl.ds(LO, 1024), :] = act2[...].astype(F32)
    columns(u7, None)

    def inner_two(r):
        rows = pl.ds(r, 256)
        acc[rows, :] = dot(u7[rows, :], w2_ref[...])

    chunks(4, 256, inner_two)

    wait(ay_in.at[pl.ds(1, 3)], ar_sem.at[1, 1])
    mine_y = pl.multiple_of(mine + y * 256, 256)
    part = wg[pl.ds(mine_y, 256), :]
    for o in range(1, YD):
        part = part + ay_in[o].astype(F32)
    wg[pl.ds(mine_y, 256), :] = part
    for o in range(1, XD):
        start = pl.multiple_of(mine_y + ((xi + o) % XD) * 64, 64)
        ax_out[o] = wg[pl.ds(start, 64), :].astype(BF16)
        push(ax_out.at[o], ax_in.at[o], ar_sem.at[2, 0], ar_sem.at[2, 1], x_dev(o))

    hop(2, 3)
    hop(3, 3)

    wait(ax_in.at[pl.ds(1, 3)], ar_sem.at[2, 1])
    mine_x = pl.multiple_of(mine_y + xi * 64, 64)
    part = wg[pl.ds(mine_x, 64), :]
    for o in range(1, XD):
        part = part + ax_in[o].astype(F32)
    az[0] = part.astype(BF16)
    for o in range(1, ZD):
        push(az.at[0], az.at[o], ar_sem.at[3, 0], ar_sem.at[3, 1], z_dev(o))

    hop(2, 4)
    hop(3, 4)

    wait(az.at[pl.ds(1, 7)], ar_sem.at[3, 1])
    total = jnp.zeros((64, 128), F32)
    for k in range(ZD):
        total = total + az[(zi - k + ZD) % ZD].astype(F32)
    fin[pl.ds(mine_x, 64), :] = total * scale
    piece = fin.at[pl.ds(mine_x, 64)]
    for o in range(1, XD):
        push(piece, piece, ag_sem.at[0, 0, o], ag_sem.at[0, 1, o], x_dev(o))

    for o in range(8):
        arrived(2, o)
    for f in range(6):
        w = w2_ref[pl.ds((f + 1) * 128, 128), :]
        for n in range(2):
            add_face(acc, n, f, dot(take_halo(2, n * 6 + f).astype(BF16), w))
    for n in range(2):
        rows = pl.ds(n * 512, 512)
        out_ref[rows, :] = ((x_ref[rows, :].astype(F32) + acc[rows, :]) * alive[n]).astype(BF16)

    for o in range(1, XD):
        start = pl.multiple_of(mine_y + ((xi - o + XD) % XD) * 64, 64)
        wait(fin.at[pl.ds(start, 64)], ag_sem.at[0, 1, o])
    piece = fin.at[pl.ds(mine_y, 256)]
    for o in range(1, YD):
        push(piece, piece, ag_sem.at[1, 0, o], ag_sem.at[1, 1, o], y_dev(o))

    for o in range(8):
        arrived(3, o)
        add_returns(3, o, o == 0)
    for f in range(6):
        w = wt1[pl.ds((f + 1) * 128, 128), :]
        for n in range(2):
            add_face(acc2, n, f, dot(ret[n * 6 + f].astype(BF16), w))
    for n in range(2):

        def grad_rows(r, n=n):
            rows = pl.ds(n * 512 + r, 256)
            grad, _ = pre_back(x_ref[rows, :].astype(F32), gain1, acc2[rows, :])
            gf_ref[rows, :] = (cot_ref[rows, :].astype(F32) * alive[n] + grad).astype(BF16)

        chunks(2, 256, grad_rows)

    for o in range(1, YD):
        start = pl.multiple_of(mine + ((y - o + YD) % YD) * 256, 256)
        wait(fin.at[pl.ds(start, 256)], ag_sem.at[1, 1, o])
    piece = fin.at[pl.ds(mine, 1024)]
    push(piece, piece, ag_sem.at[2, 0, 0], ag_sem.at[2, 1, 0], sibling)
    wait(fin.at[pl.ds(other, 1024)], ag_sem.at[2, 1, 0])
    gw1_ref[...] = fin[pl.ds(0, 896), :]
    gw2_ref[...] = fin[pl.ds(896, 896), :]
    gg1_ref[...] = fin[pl.ds(1792, 1), :]
    gg2_ref[...] = fin[pl.ds(1793, 1), :]

    for pay in range(4):
        for o in range(1, ZD):
            for b in range(2):
                wait(gath[pay][o].at[pl.ds(b * 6, 6)], ring_send.at[pay, o, b])
        for o in range(ZD):
            wait(outb.at[pay, o, pl.ds(1, 7)], x_send.at[pay, o])
    wait(tbl.at[pl.ds(1, 7)], t_sem.at[0])
    wait(ac_out, ar_sem.at[0, 0])
    wait(ay_out.at[pl.ds(1, 3)], ar_sem.at[1, 0])
    wait(ax_out.at[pl.ds(1, 3)], ar_sem.at[2, 0])
    wait(az.at[pl.ds(1, 7)], ar_sem.at[3, 0])
    for o in range(1, XD):
        wait(fin.at[pl.ds(mine_x, 64)], ag_sem.at[0, 0, o])
        wait(fin.at[pl.ds(mine_y, 256)], ag_sem.at[1, 0, o])
    wait(fin.at[pl.ds(mine, 1024)], ag_sem.at[2, 0, 0])


def shards(
    features, gain_one, weight_one, gain_two, weight_two, live, send_index, recv_index, cotangent
):
    scale = 1.0 / math.sqrt(
        features.shape[1] * features.shape[2] * lax.axis_size("shape") * lax.axis_size("space")
    )
    rows = 1024
    smem = pl.BlockSpec(memory_space=pltpu.SMEM)
    vmem = pl.BlockSpec(memory_space=pltpu.VMEM)
    results = pl.pallas_call(
        functools.partial(kernel, scale),
        out_shape=[
            jax.ShapeDtypeStruct((rows, 128), BF16),
            jax.ShapeDtypeStruct((rows, 128), BF16),
            jax.ShapeDtypeStruct((896, 128), F32),
            jax.ShapeDtypeStruct((896, 128), F32),
            jax.ShapeDtypeStruct((1, 128), F32),
            jax.ShapeDtypeStruct((1, 128), F32),
        ],
        in_specs=[smem] * 3 + [vmem] * 6,
        out_specs=[vmem] * 6,
        scratch_shapes=[
            *[pltpu.VMEM((12, 64, 128), BF16)] * 32,
            *[pltpu.VMEM((64, 64, 128), BF16)] * 4,
            pltpu.VMEM((4, 8, 8, 64, 128), BF16),
            pltpu.VMEM((8, 8, 128), jnp.int32),
            pltpu.VMEM((1040, 128), F32),
            pltpu.VMEM((512, 128), F32),
            pltpu.VMEM((rows, 896), BF16),
            pltpu.VMEM((rows, 896), BF16),
            pltpu.VMEM((rows, 128), BF16),
            pltpu.VMEM((rows, 128), BF16),
            pltpu.VMEM((rows, 128), F32),
            pltpu.VMEM((rows, 128), F32),
            pltpu.VMEM((12, 64, 128), F32),
            pltpu.VMEM((12, 64, 128), F32),
            pltpu.VMEM((12, 64, 128), F32),
            pltpu.VMEM((896, 128), BF16),
            pltpu.VMEM((896, 128), BF16),
            pltpu.VMEM((2048, 128), F32),
            pltpu.VMEM((2048, 128), F32),
            pltpu.VMEM((1024, 128), BF16),
            pltpu.VMEM((1024, 128), BF16),
            pltpu.VMEM((4, 256, 128), BF16),
            pltpu.VMEM((4, 256, 128), BF16),
            pltpu.VMEM((4, 64, 128), BF16),
            pltpu.VMEM((4, 64, 128), BF16),
            pltpu.VMEM((8, 64, 128), BF16),
            pltpu.SemaphoreType.DMA((4, 8, 2)),
            pltpu.SemaphoreType.DMA((4, 8, 2)),
            pltpu.SemaphoreType.DMA((4, 8)),
            pltpu.SemaphoreType.DMA((4, 8)),
            pltpu.SemaphoreType.DMA((2,)),
            pltpu.SemaphoreType.DMA((4, 2)),
            pltpu.SemaphoreType.DMA((3, 2, 4)),
        ],
        compiler_params=pltpu.CompilerParams(
            collective_id=0, has_side_effects=True, vmem_limit_bytes=48 * 1024 * 1024
        ),
    )(
        send_index.reshape(64),
        recv_index.reshape(12),
        live.reshape(2),
        features.reshape(rows, 128),
        gain_one.reshape(1, 128),
        weight_one.reshape(896, 128),
        gain_two.reshape(1, 128),
        weight_two.reshape(896, 128),
        cotangent.reshape(rows, 128),
    )
    out, grad, w1, w2, g1, g2 = results
    return (
        out.reshape(features.shape),
        grad.reshape(features.shape),
        w1.reshape(7, 128, 128),
        w2.reshape(7, 128, 128),
        g1.reshape(128),
        g2.reshape(128),
    )


def solution(mesh):
    bricks = P("shape", "space", None, None)
    in_specs = (
        bricks,
        P(),
        P(),
        P(),
        P(),
        P("shape", "space"),
        bricks,
        P("shape", "space", None),
        bricks,
    )
    out_specs = (bricks, bricks, P(), P(), P(), P())
    return jax.shard_map(shards, mesh=mesh, in_specs=in_specs, out_specs=out_specs, check_vma=False)
```

time: 579 us -> 115 us (0.20); the launches traced: 569 us -> 115 us
  waiting for transfers between devices: 279 us -> 0 us
  Pallas kernels: 0 us -> 105 us
  local copies, waits for them, and re-layouts: 101 us -> 9.09 us
  blocking collectives: 76 us -> 0 us
  starting transfers between devices: 37 us -> 0 us
  matrix products: 32.7 us -> 0 us
  other arithmetic: 27.2 us -> 0 us
  between operations: 15.8 us -> 0.67 us
    psum x1 -> x0, waiting for transfers between devices: 247 us -> none  [shards(): lax.psum((weight_grad_one, weight_grad_two, gain_grad_one, gain_grad_two)...]
    pallas_call x0 -> x1, Pallas kernels: none -> 105 us  [shards(): pl.pallas_call(functools.partial(kernel, scale), out_shape=[jax.ShapeDtyp...]
    psum x1 -> x0, blocking collectives: 76 us -> none  [shards(): lax.psum((weight_grad_one, weight_grad_two, gain_grad_one, gain_grad_two)...]
    unnamed x106 -> x24, local copies, waits for them, and re-layouts: 53.6 us -> 9 us
    all_to_all x4 -> x0, starting transfers between devices: 37 us -> none  [the longest x2 19.7 us: trade_faces(): lax.all_to_all(outgoing.reshape(peer_count, slot_count, -1), 'space', spl...]
    dot_general x50 -> x0, matrix products: 32.7 us -> none  [the longest x14 15.3 us: conv_back(): lax.dot_general(shifted(padded, tap_index), grad_rows, (((0,), (0,)), (()...]
    scatter-add x16 -> x0, local copies, waits for them, and re-layouts: 32.6 us -> none  [the longest x12 27.4 us: conv_back(): spread = spread.at[:, 1 + step_i:1 + step_i + edge_len, 1 + step_j:1 + st...]
    all_to_all x4 -> x0, waiting for transfers between devices: 32.5 us -> none  [the longest x2 20.6 us: return_slabs(): lax.all_to_all(outgoing.reshape(peer_count, slot_count, -1), 'space', spl...]
  transfers between devices with their start and end apart: 5 -> 0, of which waited for: 4 -> 0; matrix products, arithmetic and copies ran while one was open for 15% -> 0% of each run, Pallas kernels for 0% -> 0%
where the time goes in v1:
time: 115 us
  Pallas kernels  105 us (91%)
  local copies, waits for them, and re-layouts  9.09 us (8%)
    pallas_call x1, Pallas kernels, shards(): pl.pallas_call(functools.partial(kernel, scale), out_shape=[jax.ShapeDtyp...  105 us
    unnamed x24, local copies, waits for them, and re-layouts  9 us

profile of v1, /device:TPU:1, one launch (start us, length us, event | category | flops | bytes accessed | tf_op | source)
XLA Modules:
  0.0 114.5 jit_solution(10957661143109044843)
XLA Ops:
  0.6 0.0 copy-start.8
  0.6 0.0 copy-start.7
  0.7 0.7 copy-done.8
  1.3 0.0 copy-start.4
  1.3 0.0 copy-start.5
  1.3 0.0 copy-start.6
  1.3 0.1 reshape.58.recv_s
  1.4 0.0 copy-done.7
  1.4 0.6 copy-done.4
  2.0 0.0 copy-done.5
  2.0 0.0 copy-done.6
  2.0 0.0 copy-start
  2.0 0.9 copy-done
  3.0 0.0 copy-start.1
  3.0 0.9 copy-done.1
  3.9 0.0 copy-start.2
  3.9 0.9 copy-done.2
  4.8 0.0 copy-start.3
  4.8 0.9 copy-done.3
  5.8 104.8 %shard_map.136 = (bf16[1024,128]{1,0:T(8,128)(2,1)S(1)}, bf16[1024,128]{1,0:T(8,128)(2,1)S(1)}, f32[896,128]{1,0:T(8,128)S(1)}, f32[896,128]{1,0:T(8,128)S(1)}, ...) custom-call(s32[64]{0:T(128)S(1)} %bitcast.22, s32[12]{0:T(128)S(1)} %reshape.58.recv_s, s32[2]{0:T(128)S(1)} %bitcast.23, ...), custom_call_target="tpu_custom_call" | custom-call | tf_op jit(solution)/shard_map/pallas_call | solution.py:537
  110.6 0.7 copy.21
  111.3 0.7 copy.22
  112.0 0.8 copy.23
  112.7 0.8 copy.24
  113.5 0.5 copy.25
  114.0 0.5 copy.26
Async XLA Ops:
  0.6 0.7 copy-start.8
  0.6 0.8 copy-start.7
  1.3 0.7 copy-start.4
  1.3 0.7 copy-start.5
  1.3 0.7 copy-start.6
  2.0 0.9 copy-start
  3.0 0.9 copy-start.1
  3.9 0.9 copy-start.2
  4.8 0.9 copy-start.3

commit v2 on v1

v2 whole, which is shorter than its diff:
```python
import functools
import math

import jax
import jax.numpy as jnp
from jax import lax
from jax.experimental import pallas as pl
from jax.experimental.pallas import tpu as pltpu
from jax.sharding import PartitionSpec as P

MESH = pl.DeviceIdType.MESH
F32 = jnp.float32
BF16 = jnp.bfloat16
EPS = 1e-05
SWAP = (0, 2, 1, 4, 3, 6, 5)
XD, ZD, YD = 4, 8, 4
LO = 8
POS = (0, 1, 3, 5, 7, 6, 4, 2)
GROUPS = ((0, 3), (3, 2), (5, 2), (7, 1))


def norm(v):
    c = v - jnp.mean(v, axis=-1, keepdims=True)
    r = lax.rsqrt(jnp.mean(c * c, axis=-1, keepdims=True) + EPS)
    return c * r, r


def silu_parts(t):
    s = 1.0 / (1.0 + jnp.exp(-t))
    return t * s, s * (1.0 + t * (1.0 - s))


def rounded(v):
    return v.astype(BF16).astype(F32)


def dot(a, b):
    return jnp.dot(a, b, preferred_element_type=F32)


def dot_t(a, b):
    return lax.dot_general(a, b, (((0,), (0,)), ((), ())), preferred_element_type=F32)


def kernel(
    scale,
    send_s,
    recv_s,
    live_s,
    x_hbm,
    g1_hbm,
    w1_hbm,
    g2_hbm,
    w2_hbm,
    cot_hbm,
    out_hbm,
    gf_hbm,
    gw1_hbm,
    gw2_hbm,
    gg1_hbm,
    gg2_hbm,
    *scratch,
):
    gath = [scratch[i * 8 : i * 8 + 8] for i in range(4)]
    inb = scratch[32:36]
    (
        outb,
        tbl,
        tbl_s,
        ordv,
        ord_s,
        seg,
        col,
        fout,
        x_ref,
        cot_ref,
        w1_ref,
        w2_ref,
        gains,
        out_ref,
        gf_ref,
        a32,
        s32,
        e32,
        u7,
        v7,
        act2,
        acc,
        acc2,
        xh1,
        sl1,
        rs1,
        xh2,
        sl2,
        rs2,
        hal,
        hald,
        ret,
        wt1,
        wt2,
        wg,
        fin,
        ay_out,
        ay_in,
        ax_out,
        ax_in,
        az,
        ring_send,
        ring_recv,
        x_send,
        x_recv,
        t_sem,
        ar_sem,
        ag_sem,
        ld_sem,
        st_sem,
    ) = scratch[36:]
    y = lax.axis_index("shape")
    sp = lax.axis_index("space")
    xi = sp // 16
    zi = (sp // 2) % ZD
    ci = sp % 2

    def dev(yy, xx, zz, cc):
        return (yy, (xx * ZD + zz) * 2 + cc)

    def z_dev(o):
        return dev(y, xi, (zi + o) % ZD, ci)

    def row_dev(l, step=0):
        return dev(y, (xi + l // 2) % XD, (zi + step + ZD) % ZD, (ci + l % 2) % 2)

    def row_source(l, step):
        return dev(y, (xi - l // 2 + XD) % XD, (zi + step + ZD) % ZD, (ci + l % 2) % 2)

    def x_dev(o):
        return dev(y, (xi + o) % XD, zi, ci)

    def y_dev(j):
        return dev((y + j // 2) % YD, xi, zi, (ci + j % 2) % 2)

    barrier = pltpu.get_barrier_semaphore()

    def greet(target):
        pl.semaphore_signal(barrier, inc=1, device_id=target, device_id_type=MESH)

    for o in range(1, ZD):
        greet(z_dev(o))
    for l in range(1, 8):
        greet(row_dev(l))
    for j in range(2, 8):
        greet(y_dev(j))
    for l in range(1, 4):
        greet(row_source(l, -1))
    for l in range(4, 8):
        greet(row_source(l, 1))

    def load(src, dst, i):
        pltpu.make_async_copy(src, dst, ld_sem.at[i]).start()

    load(x_hbm, x_ref, 0)
    load(cot_hbm, cot_ref, 1)
    load(w1_hbm, w1_ref, 2)
    load(w2_hbm, w2_ref, 3)
    load(g1_hbm, gains.at[0], 4)
    load(g2_hbm, gains.at[1], 5)

    def push(src, dst, ssem, rsem, target):
        pltpu.make_async_remote_copy(
            src_ref=src,
            dst_ref=dst,
            send_sem=ssem,
            recv_sem=rsem,
            device_id=target,
            device_id_type=MESH,
        ).start()

    def wait(ref, sem):
        pltpu.make_async_copy(ref, ref, sem).wait()

    def part(pay, slot, k):
        if k == 0:
            return gath[pay][slot].at[:, pl.ds(0, 2)]
        return gath[pay][slot].at[:, pl.ds(2, 4), pl.ds(0, 48)]

    def ring(pay, src, dst, k, step):
        push(
            part(pay, src, k),
            part(pay, dst, k),
            ring_send.at[pay, dst, k],
            ring_recv.at[pay, dst, k],
            z_dev(step),
        )

    def forward(pay, h):
        for k in range(2):
            for src, dst, step in ((h, h + 1, 1), ((ZD - h) % ZD, ZD - 1 - h, ZD - 1)):
                if h > 0:
                    wait(part(pay, src, k), ring_recv.at[pay, src, k])
                if h < 3:
                    ring(pay, src, dst, k, step)

    def fill(pay, slot):
        g = gath[pay][slot]
        for n in range(2):
            e32[...] = g[n, 0:2].reshape(128, 128).astype(F32)
            g[n, 2, 48:64] = jnp.concatenate([e32[0:8], e32[64:72]], axis=0).astype(BF16)
            g[n, 3, 48:64] = jnp.concatenate([e32[56:64], e32[120:128]], axis=0).astype(BF16)
            g[n, 4, 48:64] = e32[pl.ds(0, 16, stride=8), :].astype(BF16)
            g[n, 5, 48:64] = e32[pl.ds(7, 16, stride=8), :].astype(BF16)

    def pick(pay, slot, o, l):
        code = jnp.maximum(tbl_s[slot, o, l + 8 * (pay % 2)], 0)
        slab = gath[pay][slot][code // 8, code % 8]
        if l == 0 and o == slot:
            inb[pay][0, POS[o]] = slab
        else:
            outb[pay, l, POS[o]] = slab

    def deliver(pay, group, l, step):
        first, count = GROUPS[group]
        push(
            outb.at[pay, l, pl.ds(first, count)],
            inb[pay].at[l, pl.ds(first, count)],
            x_send.at[pay, group],
            x_recv.at[pay, group],
            row_dev(l, step),
        )

    def select(pay, h):
        if h == 3:
            for l in range(4):
                pick(pay, 3, 4, l)
                deliver(pay, 3, l, 1)
            for l in range(4, 8):
                pick(pay, 5, 4, l)
                deliver(pay, 3, l, -1)
        for l in (4, 5, 2, 3, 6, 7, 1, 0):
            for o in ((0, 1, 7), (2, 6), (3, 5))[h - 1]:
                pick(pay, o, o, l)
            if l > 0:
                deliver(pay, h - 1, l, 0)

    def flying(group):
        first, count = GROUPS[group]
        return (pl.ds(0, 8) if group == 3 else pl.ds(1, 7)), pl.ds(first, count)

    def arrived(pay):
        for group in range(4):
            wait(inb[pay].at[flying(group)], x_recv.at[pay, group])

    def hop(pay, h):
        forward(pay, h)
        if h > 0:
            fill(pay, h)
            fill(pay, ZD - h)
            select(pay, h)

    def returns(pay):
        arrived(pay)

        def one(k, carry):
            total, before = carry
            v = ord_s[k, 0]
            code, at = v // 64, v % 64
            total = total * (code == before).astype(F32) + inb[pay][at // 8, at % 8].astype(F32)
            seg[k] = total
            return total, code

        lax.fori_loop(0, 64, one, (jnp.zeros((64, 128), F32), jnp.int32(-1)))

        def pickup(q, carry):
            start, end = ord_s[64 + q, 0], ord_s[65 + q, 0]
            ret[q] = seg[jnp.maximum(end - 1, 0)] * (end > start).astype(F32)
            return carry

        lax.fori_loop(0, 12, pickup, 0)

    def position(r):
        o = (zi - (r // 2) % ZD + ZD) % ZD
        l = ((xi - r // 16 + XD) % XD) * 2 + (ci + r % 2) % 2
        near = jnp.where(o < 4, jnp.maximum(2 * o - 1, 0), jnp.where(o > 4, 16 - 2 * o, 7))
        return l * 8 + near

    def take_halo(pay, q):
        r = recv_s[q // 6, q % 6]
        at = position(jnp.maximum(r, 0))
        return inb[pay][at // 8, at % 8].astype(F32) * (r >= 0).astype(F32)

    def chunks(n, size, body):
        def step(i, carry):
            body(pl.multiple_of(i * size, size))
            return carry

        lax.fori_loop(0, n, step, 0)

    def ordered(v):
        v = v.reshape(8, 8, 128)
        return jnp.concatenate([v[1:7], v[0:1], v[7:8]], axis=0).reshape(64, 128)

    def natural(v):
        v = v.reshape(8, 8, 128)
        return jnp.concatenate([v[6:7], v[0:6], v[7:8]], axis=0).reshape(64, 128)

    def faces(pay):
        g = gath[pay][0]
        for n in range(2):
            base = LO + n * 512
            cube = a32[pl.ds(base, 512), :].reshape(8, 8, 8, 128)
            g[n, 0] = a32[pl.ds(base, 64), :].astype(BF16)
            g[n, 1] = a32[pl.ds(base + 448, 64), :].astype(BF16)
            g[n, 2] = ordered(cube[:, 0]).astype(BF16)
            g[n, 3] = ordered(cube[:, 7]).astype(BF16)
            g[n, 4] = ordered(a32[pl.ds(base, 64, stride=8), :]).astype(BF16)
            g[n, 5] = ordered(a32[pl.ds(base + 7, 64, stride=8), :]).astype(BF16)

    def columns(dst):
        zero = jnp.zeros((64, 128), F32)
        plate = jnp.zeros((8, 1, 8, 128), F32)
        for n in range(2):
            base = LO + n * 512
            rows = pl.ds(n * 512, 512)
            body = a32[pl.ds(base, 512), :]
            half = body.astype(BF16)
            dst[rows, 0:128] = half
            dst[pl.ds(n * 512, 64), 128:256] = zero.astype(BF16)
            dst[pl.ds(n * 512 + 64, 448), 128:256] = half[:448]
            dst[pl.ds(n * 512, 448), 256:384] = half[64:]
            dst[pl.ds(n * 512 + 448, 64), 256:384] = zero.astype(BF16)
            cube = body.reshape(8, 8, 8, 128)
            low = jnp.concatenate([plate, cube[:, :7]], axis=1)
            dst[rows, 384:512] = low.reshape(512, 128).astype(BF16)
            high = jnp.concatenate([cube[:, 1:], plate], axis=1)
            dst[rows, 512:640] = high.reshape(512, 128).astype(BF16)
            s32[...] = a32[pl.ds(base - 1, 512), :]
            s32[pl.ds(0, 64, stride=8), :] = zero
            dst[rows, 640:768] = s32[...].astype(BF16)
            s32[...] = a32[pl.ds(base + 1, 512), :]
            s32[pl.ds(7, 64, stride=8), :] = zero
            dst[rows, 768:896] = s32[...].astype(BF16)

    def add_face(target, n, f, term):
        base = n * 512
        if f == 0:
            target[pl.ds(base, 64), :] += term
        elif f == 1:
            target[pl.ds(base + 448, 64), :] += term
        elif f < 4:
            term = natural(term)
            for i in range(8):
                target[pl.ds(base + i * 64 + (f - 2) * 56, 8), :] += term[i * 8 : i * 8 + 8]
        else:
            rows = pl.ds(base + (f - 4) * 7, 64, stride=8)
            target[rows, :] = target[rows, :] + natural(term)

    def add_faces(target, slab, w):
        for f in range(6):
            both = jnp.concatenate([slab(f), slab(6 + f)], axis=0)
            term = dot(both, w[pl.ds((f + 1) * 128, 128), :])
            add_face(target, 0, f, term[:64])
            add_face(target, 1, f, term[64:])

    def product(target, cols, w):
        def rows_of(r):
            rows = pl.ds(r, 256)
            target[rows, :] = dot(cols[rows, :], w[...])

        chunks(4, 256, rows_of)

    def back_rows(r, up, gain, xh, sl, rs):
        rows = pl.ds(r, 128)
        xhat = xh[rows, :]
        dt = up * sl[rows, :]
        d = dt * gain
        mean_d = jnp.mean(d, axis=-1, keepdims=True)
        mean_dx = jnp.mean(d * xhat, axis=-1, keepdims=True)
        return rs[rows, :] * (d - mean_d - xhat * mean_dx), dt * xhat

    def pre_rows(v, r, gain, xh, sl, rs):
        rows = pl.ds(r, 128)
        xhat, inv = norm(v)
        a, slope = silu_parts(xhat * gain)
        xh[rows, :] = xhat
        sl[rows, :] = slope
        rs[rows, :] = jnp.broadcast_to(inv, (128, 128))
        return a

    alive = [live_s[n].astype(F32) for n in range(2)]

    step_id = lax.broadcasted_iota(jnp.int32, (8, 128), 0)
    lane_id = lax.broadcasted_iota(jnp.int32, (8, 128), 1)
    in_x = lane_id % 8
    target_id = (
        ((xi + in_x // 2) % XD) * (2 * ZD) + ((zi + step_id) % ZD) * 2 + (ci + in_x % 2) % 2
    )
    codes = jnp.full((8, 128), -1, jnp.int32)
    for e in range(64):
        codes = jnp.where(target_id == e, send_s[e], codes)
    back = jnp.full((8, 128), -1, jnp.int32)
    for q in range(12):
        back = jnp.where(target_id == recv_s[q // 6, q % 6], q, back)
    chosen = jnp.where(lane_id < 8, codes, back)
    tbl[0] = chosen + 2 * (chosen >= 6).astype(jnp.int32)

    wait(x_ref, ld_sem.at[0])
    a32[pl.ds(LO, 1024), :] = x_ref[...].astype(F32)
    faces(0)
    pl.semaphore_wait(barrier, 27)
    for o in range(1, ZD):
        push(tbl.at[0], tbl.at[o], t_sem.at[0], t_sem.at[1], z_dev(o))
    forward(0, 0)

    lane = lax.broadcasted_iota(jnp.int32, (64, 128), 1)
    line = lax.broadcasted_iota(jnp.int32, (64, 128), 0)
    across = jnp.full((8, 128), 99, jnp.int32)
    for e in range(64):
        across = jnp.where(lane_id == e, send_s[e], across)
        col[pl.ds(e, 1), :] = jnp.full((1, 128), send_s[e], jnp.int32)
    across = jnp.broadcast_to(across[0:1], (64, 128))
    down = col[...]
    ahead = (down < across) | ((down == across) & (line < lane))
    rank = jnp.sum(ahead.astype(jnp.int32), axis=0, keepdims=True)
    value = position(jnp.minimum(lane, 63)) + 64 * (jnp.minimum(across, 15) + 1)
    sorted_values = jnp.sum(
        jnp.where((rank == line) & (lane < 64), value, 0), axis=1, keepdims=True
    )
    ordv[pl.ds(0, 64), :] = jnp.broadcast_to(sorted_values, (64, 128))
    below = jnp.sum((across < line).astype(jnp.int32), axis=1, keepdims=True)
    ordv[pl.ds(64, 16), :] = jnp.broadcast_to(below, (64, 128))[:16]
    pltpu.make_async_copy(ordv, ord_s, ld_sem.at[7]).start()

    wait(cot_ref, ld_sem.at[1])
    for n in range(2):
        a32[pl.ds(LO + n * 512, 512), :] = cot_ref[pl.ds(n * 512, 512), :].astype(F32) * alive[n]
    faces(1)
    columns(v7)
    wait(tbl.at[pl.ds(1, 7)], t_sem.at[1])
    codes_in = pltpu.make_async_copy(tbl, tbl_s, ld_sem.at[6])
    codes_in.start()
    codes_in.wait()
    hop(0, 1)

    wait(gains.at[0], ld_sem.at[4])
    wait(gains.at[1], ld_sem.at[5])
    gain1 = gains[0]
    gain2 = gains[1]

    def act_one(r):
        a = pre_rows(x_ref[pl.ds(r, 128), :].astype(F32), r, gain1, xh1, sl1, rs1)
        a32[pl.ds(LO + r, 128), :] = rounded(a)

    chunks(8, 128, act_one)
    hop(0, 2)
    hop(1, 0)
    columns(u7)
    wait(w1_ref, ld_sem.at[2])
    wait(w2_ref, ld_sem.at[3])
    product(acc, u7, w1_ref)
    hop(0, 3)
    for t in range(7):
        src = pl.ds(SWAP[t] * 128, 128)
        wt1[pl.ds(t * 128, 128), :] = w1_ref[src, :].astype(F32).T.astype(BF16)
        wt2[pl.ds(t * 128, 128), :] = w2_ref[src, :].astype(F32).T.astype(BF16)
    product(acc2, v7, wt2)
    hop(1, 1)

    arrived(0)

    def halo_one(q, carry):
        xhat, _ = norm(take_halo(0, q))
        act, slope = silu_parts(xhat * gain1)
        hal[q] = act.astype(BF16)
        hald[q] = slope * xhat
        return carry

    lax.fori_loop(0, 12, halo_one, 0)
    add_faces(acc, lambda q: hal[q], w1_ref)

    def hidden_rows(r):
        rows = pl.ds(r, 128)
        a = pre_rows(rounded(acc[rows, :]), r, gain2, xh2, sl2, rs2).astype(BF16)
        act2[rows, :] = a
        a32[pl.ds(LO + r, 128), :] = a.astype(F32)

    chunks(8, 128, hidden_rows)
    faces(2)
    hop(1, 2)
    hop(2, 0)

    hop(1, 3)
    hop(2, 1)
    pltpu.make_async_copy(ordv, ord_s, ld_sem.at[7]).wait()
    returns(1)
    add_faces(acc2, lambda q: ret[q].astype(BF16), wt2)
    wg[pl.ds(1792, 256), :] = jnp.zeros((256, 128), F32)

    def grad_hidden_rows(r):
        grad, per = back_rows(r, acc2[pl.ds(r, 128), :], gain2, xh2, sl2, rs2)
        a32[pl.ds(LO + r, 128), :] = rounded(grad)
        wg[pl.ds(1793, 1), :] += jnp.sum(per, axis=0, keepdims=True)

    chunks(8, 128, grad_hidden_rows)
    faces(3)
    hop(3, 0)

    def slabs(pay, f):
        return gath[pay][0][:, f].reshape(128, 128)

    a2 = act2[...]
    for t in range(7):
        total = dot_t(a2, v7[:, t * 128 : t * 128 + 128])
        if t > 0:
            r2 = jnp.concatenate([ret[t - 1], ret[t + 5]], axis=0).astype(BF16)
            total = total + dot_t(slabs(2, t - 1), r2)
        wg[pl.ds(896 + SWAP[t] * 128, 128), :] = total
    hop(2, 2)
    gh = a32[pl.ds(LO, 1024), :].astype(BF16)
    for t in range(7):
        total = dot_t(u7[:, t * 128 : t * 128 + 128], gh)
        if t > 0:
            h2 = jnp.concatenate([hal[t - 1], hal[t + 5]], axis=0)
            total = total + dot_t(h2, slabs(3, t - 1))
        wg[pl.ds(t * 128, 128), :] = total

    columns(v7)
    product(acc2, v7, wt1)

    def gain_rows(r):
        rows = pl.ds(r, 128)
        per = acc2[rows, :] * sl1[rows, :] * xh1[rows, :]
        wg[pl.ds(1792, 1), :] += jnp.sum(per, axis=0, keepdims=True)

    chunks(8, 128, gain_rows)
    for f in range(6):
        both = dot(slabs(3, f), wt1[pl.ds(SWAP[f + 1] * 128, 128), :])
        slope = jnp.concatenate([hald[f], hald[6 + f]], axis=0)
        wg[pl.ds(1792, 1), :] += jnp.sum(rounded(both) * slope, axis=0, keepdims=True)

    mine = pl.multiple_of(ci * 1024 + y * 256, 256)
    for j in range(1, 8):
        start = pl.multiple_of((ci + j % 2) % 2 * 1024 + (y + j // 2) % YD * 256, 256)
        ay_out[j] = wg[pl.ds(start, 256), :].astype(BF16)
        push(ay_out.at[j], ay_in.at[j], ar_sem.at[0, 0], ar_sem.at[0, 1], y_dev(j))

    hop(3, 1)
    hop(2, 3)

    a32[pl.ds(LO, 1024), :] = act2[...].astype(F32)
    columns(u7)
    product(acc, u7, w2_ref)

    wait(ay_in.at[pl.ds(1, 7)], ar_sem.at[0, 1])
    partial = wg[pl.ds(mine, 256), :]
    for j in range(1, 8):
        partial = partial + ay_in[j].astype(F32)
    wg[pl.ds(mine, 256), :] = partial
    for o in range(1, XD):
        start = pl.multiple_of(mine + ((xi + o) % XD) * 64, 64)
        ax_out[o] = wg[pl.ds(start, 64), :].astype(BF16)
        push(ax_out.at[o], ax_in.at[o], ar_sem.at[1, 0], ar_sem.at[1, 1], x_dev(o))

    hop(3, 2)

    wait(ax_in.at[pl.ds(1, 3)], ar_sem.at[1, 1])
    mine_x = pl.multiple_of(mine + xi * 64, 64)
    partial = wg[pl.ds(mine_x, 64), :]
    for o in range(1, XD):
        partial = partial + ax_in[o].astype(F32)
    az[0] = partial.astype(BF16)
    for o in range(1, ZD):
        push(az.at[0], az.at[o], ar_sem.at[2, 0], ar_sem.at[2, 1], z_dev(o))

    arrived(2)
    add_faces(acc, lambda q: take_halo(2, q).astype(BF16), w2_ref)
    for n in range(2):
        rows = pl.ds(n * 512, 512)
        out_ref[rows, :] = ((x_ref[rows, :].astype(F32) + acc[rows, :]) * alive[n]).astype(BF16)

    def store(src, dst, i):
        pltpu.make_async_copy(src, dst, st_sem.at[i]).start()

    store(out_ref, out_hbm, 0)

    wait(az.at[pl.ds(1, 7)], ar_sem.at[2, 1])
    total = jnp.zeros((64, 128), F32)
    for k in range(ZD):
        total = total + az[(zi - k + ZD) % ZD].astype(F32)
    fin[pl.ds(mine_x, 64), :] = (total * scale).astype(BF16)
    piece = fin.at[pl.ds(mine_x, 64)]
    for o in range(1, XD):
        push(piece, piece, ag_sem.at[0, 0, o], ag_sem.at[0, 1, o], x_dev(o))

    hop(3, 3)

    for o in range(1, XD):
        start = pl.multiple_of(mine + ((xi - o + XD) % XD) * 64, 64)
        wait(fin.at[pl.ds(start, 64)], ag_sem.at[0, 1, o])
    piece = fin.at[pl.ds(mine, 256)]
    for j in range(1, 8):
        push(piece, piece, ag_sem.at[1, 0, j], ag_sem.at[1, 1, j], y_dev(j))

    returns(3)
    add_faces(acc2, lambda q: ret[q].astype(BF16), wt1)
    for n in range(2):

        def grad_rows(i, n=n):
            r = pl.multiple_of(n * 512 + i, 128)
            rows = pl.ds(r, 128)
            grad, _ = back_rows(r, acc2[rows, :], gain1, xh1, sl1, rs1)
            gf_ref[rows, :] = (cot_ref[rows, :].astype(F32) * alive[n] + grad).astype(BF16)

        chunks(4, 128, grad_rows)
    store(gf_ref, gf_hbm, 1)

    for j in range(1, 8):
        start = pl.multiple_of((ci + j % 2) % 2 * 1024 + (y - j // 2 + YD) % YD * 256, 256)
        wait(fin.at[pl.ds(start, 256)], ag_sem.at[1, 1, j])
    fout[...] = fin[pl.ds(0, 1808), :].astype(F32)
    store(fout.at[pl.ds(0, 896)], gw1_hbm, 2)
    store(fout.at[pl.ds(896, 896)], gw2_hbm, 3)
    store(fout.at[pl.ds(1792, 1)], gg1_hbm, 4)
    store(fout.at[pl.ds(1793, 1)], gg2_hbm, 5)

    for pay in range(4):
        for o in (1, 2, 3, 5, 6, 7):
            for k in range(2):
                wait(part(pay, o, k), ring_send.at[pay, o, k])
        for group in range(4):
            wait(outb.at[(pay, *flying(group))], x_send.at[pay, group])
    wait(tbl.at[pl.ds(1, 7)], t_sem.at[0])
    wait(ay_out.at[pl.ds(1, 7)], ar_sem.at[0, 0])
    wait(ax_out.at[pl.ds(1, 3)], ar_sem.at[1, 0])
    wait(az.at[pl.ds(1, 7)], ar_sem.at[2, 0])
    for o in range(1, XD):
        wait(fin.at[pl.ds(mine_x, 64)], ag_sem.at[0, 0, o])
    for j in range(1, 8):
        wait(fin.at[pl.ds(mine, 256)], ag_sem.at[1, 0, j])
    for i, ref in enumerate((out_ref, gf_ref)):
        wait(ref, st_sem.at[i])
    for i in range(2):
        wait(fout.at[pl.ds(0, 896)], st_sem.at[2 + i])
        wait(fout.at[pl.ds(1792, 1)], st_sem.at[4 + i])


def hand_over(*refs):
    sems = refs[18]
    loads = [pltpu.make_async_copy(refs[i], refs[12 + i], sems.at[0, i]) for i in range(6)]
    stores = [pltpu.make_async_copy(refs[12 + i], refs[6 + i], sems.at[1, i]) for i in range(6)]
    for copy in loads:
        copy.start()
    for copy, store in zip(loads, stores):
        copy.wait()
        store.start()
    for store in stores:
        store.wait()


def shards(
    features, gain_one, weight_one, gain_two, weight_two, live, send_index, recv_index, cotangent
):
    scale = 1.0 / math.sqrt(
        features.shape[1] * features.shape[2] * lax.axis_size("shape") * lax.axis_size("space")
    )
    rows = 1024
    smem = pl.BlockSpec(memory_space=pltpu.SMEM)
    hbm = pl.BlockSpec(memory_space=pltpu.HBM)
    shapes = [
        jax.ShapeDtypeStruct((rows, 128), BF16),
        jax.ShapeDtypeStruct((rows, 128), BF16),
        jax.ShapeDtypeStruct((896, 128), F32),
        jax.ShapeDtypeStruct((896, 128), F32),
        jax.ShapeDtypeStruct((1, 128), F32),
        jax.ShapeDtypeStruct((1, 128), F32),
    ]
    results = pl.pallas_call(
        functools.partial(kernel, scale),
        out_shape=shapes,
        in_specs=[smem] * 3 + [hbm] * 6,
        out_specs=[hbm] * 6,
        scratch_shapes=[
            *[pltpu.VMEM((2, 6, 64, 128), BF16)] * 32,
            *[pltpu.VMEM((8, 8, 64, 128), BF16)] * 4,
            pltpu.VMEM((4, 8, 8, 64, 128), BF16),
            pltpu.VMEM((8, 8, 128), jnp.int32),
            pltpu.SMEM((8, 8, 128), jnp.int32),
            pltpu.VMEM((80, 128), jnp.int32),
            pltpu.SMEM((80, 128), jnp.int32),
            pltpu.VMEM((64, 64, 128), F32),
            pltpu.VMEM((64, 128), jnp.int32),
            pltpu.VMEM((1808, 128), F32),
            pltpu.VMEM((rows, 128), BF16),
            pltpu.VMEM((rows, 128), BF16),
            pltpu.VMEM((896, 128), BF16),
            pltpu.VMEM((896, 128), BF16),
            pltpu.VMEM((2, 1, 128), F32),
            pltpu.VMEM((rows, 128), BF16),
            pltpu.VMEM((rows, 128), BF16),
            pltpu.VMEM((1040, 128), F32),
            pltpu.VMEM((512, 128), F32),
            pltpu.VMEM((128, 128), F32),
            pltpu.VMEM((rows, 896), BF16),
            pltpu.VMEM((rows, 896), BF16),
            pltpu.VMEM((rows, 128), BF16),
            *[pltpu.VMEM((rows, 128), F32)] * 8,
            pltpu.VMEM((12, 64, 128), BF16),
            pltpu.VMEM((12, 64, 128), F32),
            pltpu.VMEM((12, 64, 128), F32),
            pltpu.VMEM((896, 128), BF16),
            pltpu.VMEM((896, 128), BF16),
            pltpu.VMEM((2048, 128), F32),
            pltpu.VMEM((2048, 128), BF16),
            pltpu.VMEM((8, 256, 128), BF16),
            pltpu.VMEM((8, 256, 128), BF16),
            pltpu.VMEM((4, 64, 128), BF16),
            pltpu.VMEM((4, 64, 128), BF16),
            pltpu.VMEM((8, 64, 128), BF16),
            pltpu.SemaphoreType.DMA((4, 8, 2)),
            pltpu.SemaphoreType.DMA((4, 8, 2)),
            pltpu.SemaphoreType.DMA((4, 4)),
            pltpu.SemaphoreType.DMA((4, 4)),
            pltpu.SemaphoreType.DMA((2,)),
            pltpu.SemaphoreType.DMA((3, 2)),
            pltpu.SemaphoreType.DMA((2, 2, 8)),
            pltpu.SemaphoreType.DMA((8,)),
            pltpu.SemaphoreType.DMA((6,)),
        ],
        compiler_params=pltpu.CompilerParams(
            collective_id=0, has_side_effects=True, vmem_limit_bytes=56 * 1024 * 1024
        ),
    )(
        send_index.reshape(64),
        recv_index.reshape(2, 6),
        live.reshape(2),
        features.reshape(rows, 128),
        gain_one.reshape(1, 128),
        weight_one.reshape(896, 128),
        gain_two.reshape(1, 128),
        weight_two.reshape(896, 128),
        cotangent.reshape(rows, 128),
    )
    out, grad, w1, w2, g1, g2 = pl.pallas_call(
        hand_over,
        out_shape=shapes,
        in_specs=[hbm] * 6,
        out_specs=[hbm] * 6,
        scratch_shapes=[
            *[pltpu.VMEM(s.shape, s.dtype) for s in shapes],
            pltpu.SemaphoreType.DMA((2, 6)),
        ],
    )(*results)
    return (
        out.reshape(features.shape),
        grad.reshape(features.shape),
        w1.reshape(7, 128, 128),
        w2.reshape(7, 128, 128),
        g1.reshape(128),
        g2.reshape(128),
    )


def solution(mesh):
    bricks = P("shape", "space", None, None)
    in_specs = (
        bricks,
        P(),
        P(),
        P(),
        P(),
        P("shape", "space"),
        bricks,
        P("shape", "space", None),
        bricks,
    )
    out_specs = (bricks, bricks, P(), P(), P(), P())
    return jax.shard_map(shards, mesh=mesh, in_specs=in_specs, out_specs=out_specs, check_vma=False)
```

time: 115 us -> 97.3 us (0.85)
  local copies, waits for them, and re-layouts: 9.09 us -> 0 us
  Pallas kernels: 105 us -> 96.5 us
    unnamed x24 -> x0, local copies, waits for them, and re-layouts: 9 us -> none
    pallas_call x1 -> x2, Pallas kernels: 105 us -> 96.5 us  [the longest x1 94.3 us: shards(): pl.pallas_call(functools.partial(kernel, scale), out_shape=shapes, in_spe...]
where the time goes in v2:
time: 97.3 us; the launch traced here: 97.1 us
  Pallas kernels  96.5 us (99%)
    pallas_call x1, Pallas kernels, shards(): pl.pallas_call(functools.partial(kernel, scale), out_shape=shapes, in_spe...  94.3 us
    pallas_call x1, Pallas kernels, shards(): pl.pallas_call(hand_over, out_shape=shapes, in_specs=[hbm] * 6, out_specs...  2.21 us

profile of v2, /device:TPU:1, one launch (start us, length us, event | category | flops | bytes accessed | tf_op | source)
XLA Modules:
  0.0 97.1 jit_solution(4519829584624452556)
XLA Ops:
  0.6 94.3 %shard_map.136 = (bf16[1024,128]{1,0:T(8,128)(2,1)}, bf16[1024,128]{1,0:T(8,128)(2,1)}, f32[896,128]{1,0:T(8,128)}, f32[896,128]{1,0:T(8,128)}, f32[1,128]{1,0:T(1,128)}, /*index=5*/f32[1,128]{1,0:T(1,128)}) custom-call(s32[64]{0:T(128)} %bitcast.20, s32[2,6]{1,0:T(2,128)} %bitcast.19, s32[2]{0:T(128)} %bitcast.21, bf16[1024,128]{1,0:T(8,128)(2,1)} %bitcast.15, ...), custom_call_target="tpu_custom_call" | custom-call | tf_op jit(solution)/shard_map/pallas_call | solution.py:675
  94.9 2.2 %shard_map.137 = (bf16[1024,128]{1,0:T(8,128)(2,1)}, bf16[1024,128]{1,0:T(8,128)(2,1)}, f32[896,128]{1,0:T(8,128)}, f32[896,128]{1,0:T(8,128)}, f32[1,128]{1,0:T(1,128)}, /*index=5*/f32[1,128]{1,0:T(1,128)}) custom-call(bf16[1024,128]{1,0:T(8,128)(2,1)} %get-tuple-element.18.refs_0_, bf16[1024,128]{1,0:T(8,128)(2,1)} %get-tuple-element.19.refs_1_, ...), custom_call_target="tpu_custom_call" | custom-call | tf_op jit(solution)/shard_map/pallas_call | solution.py:741

commit v3 on v2

--- a/solution.py
+++ b/solution.py
@@ -15,6 +15,9 @@
 SWAP = (0, 2, 1, 4, 3, 6, 5)
 XD, ZD, YD = 4, 8, 4
 LO = 8
+UNH = 4
+UNC = 4
+UNP = 4
 POS = (0, 1, 3, 5, 7, 6, 4, 2)
 GROUPS = ((0, 3), (3, 2), (5, 2), (7, 1))
 
@@ -26,7 +29,7 @@
 
 
 def silu_parts(t):
-    s = 1.0 / (1.0 + jnp.exp(-t))
+    s = 0.5 * jnp.tanh(0.5 * t) + 0.5
     return t * s, s * (1.0 + t * (1.0 - s))
 
 
@@ -100,6 +103,8 @@
         wt2,
         wg,
         fin,
+        ac_out,
+        ac_in,
         ay_out,
         ay_in,
         ax_out,
@@ -136,8 +141,8 @@
     def x_dev(o):
         return dev(y, (xi + o) % XD, zi, ci)
 
-    def y_dev(j):
-        return dev((y + j // 2) % YD, xi, zi, (ci + j % 2) % 2)
+    def y_dev(o):
+        return dev((y + o) % YD, xi, zi, ci)
 
     barrier = pltpu.get_barrier_semaphore()
 
@@ -148,8 +153,8 @@
         greet(z_dev(o))
     for l in range(1, 8):
         greet(row_dev(l))
-    for j in range(2, 8):
-        greet(y_dev(j))
+    for o in range(1, YD):
+        greet(y_dev(o))
     for l in range(1, 4):
         greet(row_source(l, -1))
     for l in range(4, 8):
@@ -267,14 +272,14 @@
             seg[k] = total
             return total, code
 
-        lax.fori_loop(0, 64, one, (jnp.zeros((64, 128), F32), jnp.int32(-1)))
+        lax.fori_loop(0, 64, one, (jnp.zeros((64, 128), F32), jnp.int32(-1)), unroll=8)
 
         def pickup(q, carry):
             start, end = ord_s[64 + q, 0], ord_s[65 + q, 0]
             ret[q] = seg[jnp.maximum(end - 1, 0)] * (end > start).astype(F32)
             return carry
 
-        lax.fori_loop(0, 12, pickup, 0)
+        lax.fori_loop(0, 12, pickup, 0, unroll=4)
 
     def position(r):
         o = (zi - (r // 2) % ZD + ZD) % ZD
@@ -292,7 +297,7 @@
             body(pl.multiple_of(i * size, size))
             return carry
 
-        lax.fori_loop(0, n, step, 0)
+        lax.fori_loop(0, n, step, 0, unroll=UNC if size == 128 else UNP)
 
     def ordered(v):
         v = v.reshape(8, 8, 128)
@@ -405,7 +410,7 @@
     wait(x_ref, ld_sem.at[0])
     a32[pl.ds(LO, 1024), :] = x_ref[...].astype(F32)
     faces(0)
-    pl.semaphore_wait(barrier, 27)
+    pl.semaphore_wait(barrier, 24)
     for o in range(1, ZD):
         push(tbl.at[0], tbl.at[o], t_sem.at[0], t_sem.at[1], z_dev(o))
     forward(0, 0)
@@ -473,7 +478,7 @@
         hald[q] = slope * xhat
         return carry
 
-    lax.fori_loop(0, 12, halo_one, 0)
+    lax.fori_loop(0, 12, halo_one, 0, unroll=UNH)
     add_faces(acc, lambda q: hal[q], w1_ref)
 
     def hidden_rows(r):
@@ -502,6 +507,7 @@
     chunks(8, 128, grad_hidden_rows)
     faces(3)
     hop(3, 0)
+    hop(2, 2)
 
     def slabs(pay, f):
         return gath[pay][0][:, f].reshape(128, 128)
@@ -513,7 +519,6 @@
             r2 = jnp.concatenate([ret[t - 1], ret[t + 5]], axis=0).astype(BF16)
             total = total + dot_t(slabs(2, t - 1), r2)
         wg[pl.ds(896 + SWAP[t] * 128, 128), :] = total
-    hop(2, 2)
     gh = a32[pl.ds(LO, 1024), :].astype(BF16)
     for t in range(7):
         total = dot_t(u7[:, t * 128 : t * 128 + 128], gh)
@@ -536,23 +541,29 @@
         slope = jnp.concatenate([hald[f], hald[6 + f]], axis=0)
         wg[pl.ds(1792, 1), :] += jnp.sum(rounded(both) * slope, axis=0, keepdims=True)
 
-    mine = pl.multiple_of(ci * 1024 + y * 256, 256)
-    for j in range(1, 8):
-        start = pl.multiple_of((ci + j % 2) % 2 * 1024 + (y + j // 2) % YD * 256, 256)
-        ay_out[j] = wg[pl.ds(start, 256), :].astype(BF16)
-        push(ay_out.at[j], ay_in.at[j], ar_sem.at[0, 0], ar_sem.at[0, 1], y_dev(j))
+    half = pl.multiple_of(ci * 1024, 1024)
+    other = pl.multiple_of((1 - ci) * 1024, 1024)
+    mine = pl.multiple_of(half + y * 256, 256)
+    ac_out[...] = wg[pl.ds(other, 1024), :].astype(BF16)
+    push(ac_out, ac_in, ar_sem.at[3, 0], ar_sem.at[3, 1], row_dev(1))
 
     hop(3, 1)
+    wait(ac_in, ar_sem.at[3, 1])
+    wg[pl.ds(half, 1024), :] += ac_in[...].astype(F32)
+    for o in range(1, YD):
+        start = pl.multiple_of(half + (y + o) % YD * 256, 256)
+        ay_out[o] = wg[pl.ds(start, 256), :].astype(BF16)
+        push(ay_out.at[o], ay_in.at[o], ar_sem.at[0, 0], ar_sem.at[0, 1], y_dev(o))
     hop(2, 3)
 
     a32[pl.ds(LO, 1024), :] = act2[...].astype(F32)
     columns(u7)
     product(acc, u7, w2_ref)
 
-    wait(ay_in.at[pl.ds(1, 7)], ar_sem.at[0, 1])
+    wait(ay_in.at[pl.ds(1, 3)], ar_sem.at[0, 1])
     partial = wg[pl.ds(mine, 256), :]
-    for j in range(1, 8):
-        partial = partial + ay_in[j].astype(F32)
+    for o in range(1, YD):
+        partial = partial + ay_in[o].astype(F32)
     wg[pl.ds(mine, 256), :] = partial
     for o in range(1, XD):
         start = pl.multiple_of(mine + ((xi + o) % XD) * 64, 64)
@@ -581,6 +592,7 @@
 
     store(out_ref, out_hbm, 0)
 
+    hop(3, 3)
     wait(az.at[pl.ds(1, 7)], ar_sem.at[2, 1])
     total = jnp.zeros((64, 128), F32)
     for k in range(ZD):
@@ -590,16 +602,16 @@
     for o in range(1, XD):
         push(piece, piece, ag_sem.at[0, 0, o], ag_sem.at[0, 1, o], x_dev(o))
 
-    hop(3, 3)
-
-    for o in range(1, XD):
-        start = pl.multiple_of(mine + ((xi - o + XD) % XD) * 64, 64)
-        wait(fin.at[pl.ds(start, 64)], ag_sem.at[0, 1, o])
-    piece = fin.at[pl.ds(mine, 256)]
-    for j in range(1, 8):
-        push(piece, piece, ag_sem.at[1, 0, j], ag_sem.at[1, 1, j], y_dev(j))
+    def gather_y():
+        for o in range(1, XD):
+            start = pl.multiple_of(mine + ((xi - o + XD) % XD) * 64, 64)
+            wait(fin.at[pl.ds(start, 64)], ag_sem.at[0, 1, o])
+        piece = fin.at[pl.ds(mine, 256)]
+        for o in range(1, YD):
+            push(piece, piece, ag_sem.at[1, 0, o], ag_sem.at[1, 1, o], y_dev(o))
 
     returns(3)
+    gather_y()
     add_faces(acc2, lambda q: ret[q].astype(BF16), wt1)
     for n in range(2):
 
@@ -612,9 +624,12 @@
         chunks(4, 128, grad_rows)
     store(gf_ref, gf_hbm, 1)
 
-    for j in range(1, 8):
-        start = pl.multiple_of((ci + j % 2) % 2 * 1024 + (y - j // 2 + YD) % YD * 256, 256)
-        wait(fin.at[pl.ds(start, 256)], ag_sem.at[1, 1, j])
+    for o in range(1, YD):
+        start = pl.multiple_of(half + (y - o + YD) % YD * 256, 256)
+        wait(fin.at[pl.ds(start, 256)], ag_sem.at[1, 1, o])
+    piece = fin.at[pl.ds(half, 1024)]
+    push(piece, piece, ag_sem.at[2, 0, 0], ag_sem.at[2, 1, 0], row_dev(1))
+    wait(fin.at[pl.ds(other, 1024)], ag_sem.at[2, 1, 0])
     fout[...] = fin[pl.ds(0, 1808), :].astype(F32)
     store(fout.at[pl.ds(0, 896)], gw1_hbm, 2)
     store(fout.at[pl.ds(896, 896)], gw2_hbm, 3)
@@ -628,13 +643,15 @@
         for group in range(4):
             wait(outb.at[(pay, *flying(group))], x_send.at[pay, group])
     wait(tbl.at[pl.ds(1, 7)], t_sem.at[0])
-    wait(ay_out.at[pl.ds(1, 7)], ar_sem.at[0, 0])
+    wait(ac_out, ar_sem.at[3, 0])
+    wait(ay_out.at[pl.ds(1, 3)], ar_sem.at[0, 0])
     wait(ax_out.at[pl.ds(1, 3)], ar_sem.at[1, 0])
     wait(az.at[pl.ds(1, 7)], ar_sem.at[2, 0])
     for o in range(1, XD):
         wait(fin.at[pl.ds(mine_x, 64)], ag_sem.at[0, 0, o])
-    for j in range(1, 8):
-        wait(fin.at[pl.ds(mine, 256)], ag_sem.at[1, 0, j])
+    for o in range(1, YD):
+        wait(fin.at[pl.ds(mine, 256)], ag_sem.at[1, 0, o])
+    wait(fin.at[pl.ds(half, 1024)], ag_sem.at[2, 0, 0])
     for i, ref in enumerate((out_ref, gf_ref)):
         wait(ref, st_sem.at[i])
     for i in range(2):
@@ -709,8 +726,10 @@
             pltpu.VMEM((896, 128), BF16),
             pltpu.VMEM((2048, 128), F32),
             pltpu.VMEM((2048, 128), BF16),
-            pltpu.VMEM((8, 256, 128), BF16),
-            pltpu.VMEM((8, 256, 128), BF16),
+            pltpu.VMEM((1024, 128), BF16),
+            pltpu.VMEM((1024, 128), BF16),
+            pltpu.VMEM((4, 256, 128), BF16),
+            pltpu.VMEM((4, 256, 128), BF16),
             pltpu.VMEM((4, 64, 128), BF16),
             pltpu.VMEM((4, 64, 128), BF16),
             pltpu.VMEM((8, 64, 128), BF16),
@@ -719,8 +738,8 @@
             pltpu.SemaphoreType.DMA((4, 4)),
             pltpu.SemaphoreType.DMA((4, 4)),
             pltpu.SemaphoreType.DMA((2,)),
-            pltpu.SemaphoreType.DMA((3, 2)),
-            pltpu.SemaphoreType.DMA((2, 2, 8)),
+            pltpu.SemaphoreType.DMA((4, 2)),
+            pltpu.SemaphoreType.DMA((3, 2, 4)),
             pltpu.SemaphoreType.DMA((8,)),
             pltpu.SemaphoreType.DMA((6,)),
         ],

time: 97.3 us -> 91.4 us (0.939)
  Pallas kernels: 96.5 us -> 90.6 us
    pallas_call x1, Pallas kernels: 94.3 us -> 88.4 us  [shards(): pl.pallas_call(functools.partial(kernel, scale), out_shape=shapes, in_spe...]
where the time goes in v3:
time: 91.4 us; the launch traced here: 91.2 us
  Pallas kernels  90.6 us (99%)
    pallas_call x1, Pallas kernels, shards(): pl.pallas_call(functools.partial(kernel, scale), out_shape=shapes, in_spe...  88.4 us
    pallas_call x1, Pallas kernels, shards(): pl.pallas_call(hand_over, out_shape=shapes, in_specs=[hbm] * 6, out_specs...  2.21 us

profile of v3, /device:TPU:1, one launch (start us, length us, event | category | flops | bytes accessed | tf_op | source)
XLA Modules:
  0.0 91.2 jit_solution(6219262725150302040)
XLA Ops:
  0.6 88.4 %shard_map.136 = (bf16[1024,128]{1,0:T(8,128)(2,1)}, bf16[1024,128]{1,0:T(8,128)(2,1)}, f32[896,128]{1,0:T(8,128)}, f32[896,128]{1,0:T(8,128)}, f32[1,128]{1,0:T(1,128)}, /*index=5*/f32[1,128]{1,0:T(1,128)}) custom-call(s32[64]{0:T(128)} %bitcast.20, s32[2,6]{1,0:T(2,128)} %bitcast.19, s32[2]{0:T(128)} %bitcast.21, bf16[1024,128]{1,0:T(8,128)(2,1)} %bitcast.15, ...), custom_call_target="tpu_custom_call" | custom-call | tf_op jit(solution)/shard_map/pallas_call | solution.py:692
  89.0 2.2 %shard_map.137 = (bf16[1024,128]{1,0:T(8,128)(2,1)}, bf16[1024,128]{1,0:T(8,128)(2,1)}, f32[896,128]{1,0:T(8,128)}, f32[896,128]{1,0:T(8,128)}, f32[1,128]{1,0:T(1,128)}, /*index=5*/f32[1,128]{1,0:T(1,128)}) custom-call(bf16[1024,128]{1,0:T(8,128)(2,1)} %get-tuple-element.18.refs_0_, bf16[1024,128]{1,0:T(8,128)(2,1)} %get-tuple-element.19.refs_1_, ...), custom_call_target="tpu_custom_call" | custom-call | tf_op jit(solution)/shard_map/pallas_call | solution.py:760

commit v4 on v3

--- a/solution.py
+++ b/solution.py
@@ -56,12 +56,12 @@
     g2_hbm,
     w2_hbm,
     cot_hbm,
-    out_hbm,
-    gf_hbm,
-    gw1_hbm,
-    gw2_hbm,
-    gg1_hbm,
-    gg2_hbm,
+    out_ref,
+    gf_ref,
+    gw1_ref,
+    gw2_ref,
+    gg1_ref,
+    gg2_ref,
     *scratch,
 ):
     gath = [scratch[i * 8 : i * 8 + 8] for i in range(4)]
@@ -74,14 +74,11 @@
         ord_s,
         seg,
         col,
-        fout,
         x_ref,
         cot_ref,
         w1_ref,
         w2_ref,
         gains,
-        out_ref,
-        gf_ref,
         a32,
         s32,
         e32,
@@ -118,7 +115,6 @@
         ar_sem,
         ag_sem,
         ld_sem,
-        st_sem,
     ) = scratch[36:]
     y = lax.axis_index("shape")
     sp = lax.axis_index("space")
@@ -547,13 +543,13 @@
     ac_out[...] = wg[pl.ds(other, 1024), :].astype(BF16)
     push(ac_out, ac_in, ar_sem.at[3, 0], ar_sem.at[3, 1], row_dev(1))
 
-    hop(3, 1)
     wait(ac_in, ar_sem.at[3, 1])
     wg[pl.ds(half, 1024), :] += ac_in[...].astype(F32)
     for o in range(1, YD):
         start = pl.multiple_of(half + (y + o) % YD * 256, 256)
         ay_out[o] = wg[pl.ds(start, 256), :].astype(BF16)
         push(ay_out.at[o], ay_in.at[o], ar_sem.at[0, 0], ar_sem.at[0, 1], y_dev(o))
+    hop(3, 1)
     hop(2, 3)
 
     a32[pl.ds(LO, 1024), :] = act2[...].astype(F32)
@@ -570,7 +566,12 @@
         ax_out[o] = wg[pl.ds(start, 64), :].astype(BF16)
         push(ax_out.at[o], ax_in.at[o], ar_sem.at[1, 0], ar_sem.at[1, 1], x_dev(o))
 
-    hop(3, 2)
+    arrived(2)
+    add_faces(acc, lambda q: take_halo(2, q).astype(BF16), w2_ref)
+    for n in range(2):
+        rows = pl.ds(n * 512, 512)
+        out_ref[rows, :] = ((x_ref[rows, :].astype(F32) + acc[rows, :]) * alive[n]).astype(BF16)
+
 
     wait(ax_in.at[pl.ds(1, 3)], ar_sem.at[1, 1])
     mine_x = pl.multiple_of(mine + xi * 64, 64)
@@ -581,18 +582,7 @@
     for o in range(1, ZD):
         push(az.at[0], az.at[o], ar_sem.at[2, 0], ar_sem.at[2, 1], z_dev(o))
 
-    arrived(2)
-    add_faces(acc, lambda q: take_halo(2, q).astype(BF16), w2_ref)
-    for n in range(2):
-        rows = pl.ds(n * 512, 512)
-        out_ref[rows, :] = ((x_ref[rows, :].astype(F32) + acc[rows, :]) * alive[n]).astype(BF16)
-
-    def store(src, dst, i):
-        pltpu.make_async_copy(src, dst, st_sem.at[i]).start()
-
-    store(out_ref, out_hbm, 0)
-
-    hop(3, 3)
+    hop(3, 2)
     wait(az.at[pl.ds(1, 7)], ar_sem.at[2, 1])
     total = jnp.zeros((64, 128), F32)
     for k in range(ZD):
@@ -602,6 +592,8 @@
     for o in range(1, XD):
         push(piece, piece, ag_sem.at[0, 0, o], ag_sem.at[0, 1, o], x_dev(o))
 
+    hop(3, 3)
+
     def gather_y():
         for o in range(1, XD):
             start = pl.multiple_of(mine + ((xi - o + XD) % XD) * 64, 64)
@@ -610,8 +602,13 @@
         for o in range(1, YD):
             push(piece, piece, ag_sem.at[1, 0, o], ag_sem.at[1, 1, o], y_dev(o))
 
+    gather_y()
     returns(3)
-    gather_y()
+    for o in range(1, YD):
+        start = pl.multiple_of(half + (y - o + YD) % YD * 256, 256)
+        wait(fin.at[pl.ds(start, 256)], ag_sem.at[1, 1, o])
+    piece = fin.at[pl.ds(half, 1024)]
+    push(piece, piece, ag_sem.at[2, 0, 0], ag_sem.at[2, 1, 0], row_dev(1))
     add_faces(acc2, lambda q: ret[q].astype(BF16), wt1)
     for n in range(2):
 
@@ -622,19 +619,13 @@
             gf_ref[rows, :] = (cot_ref[rows, :].astype(F32) * alive[n] + grad).astype(BF16)
 
         chunks(4, 128, grad_rows)
-    store(gf_ref, gf_hbm, 1)
-
-    for o in range(1, YD):
-        start = pl.multiple_of(half + (y - o + YD) % YD * 256, 256)
-        wait(fin.at[pl.ds(start, 256)], ag_sem.at[1, 1, o])
-    piece = fin.at[pl.ds(half, 1024)]
-    push(piece, piece, ag_sem.at[2, 0, 0], ag_sem.at[2, 1, 0], row_dev(1))
+
     wait(fin.at[pl.ds(other, 1024)], ag_sem.at[2, 1, 0])
-    fout[...] = fin[pl.ds(0, 1808), :].astype(F32)
-    store(fout.at[pl.ds(0, 896)], gw1_hbm, 2)
-    store(fout.at[pl.ds(896, 896)], gw2_hbm, 3)
-    store(fout.at[pl.ds(1792, 1)], gg1_hbm, 4)
-    store(fout.at[pl.ds(1793, 1)], gg2_hbm, 5)
+    gw1_ref[...] = fin[pl.ds(0, 896), :].astype(F32)
+    gw2_ref[...] = fin[pl.ds(896, 896), :].astype(F32)
+    last = fin[pl.ds(1792, 16), :].astype(F32)
+    gg1_ref[...] = last[0:1]
+    gg2_ref[...] = last[1:2]
 
     for pay in range(4):
         for o in (1, 2, 3, 5, 6, 7):
@@ -652,21 +643,12 @@
     for o in range(1, YD):
         wait(fin.at[pl.ds(mine, 256)], ag_sem.at[1, 0, o])
     wait(fin.at[pl.ds(half, 1024)], ag_sem.at[2, 0, 0])
-    for i, ref in enumerate((out_ref, gf_ref)):
-        wait(ref, st_sem.at[i])
-    for i in range(2):
-        wait(fout.at[pl.ds(0, 896)], st_sem.at[2 + i])
-        wait(fout.at[pl.ds(1792, 1)], st_sem.at[4 + i])
 
 
 def hand_over(*refs):
-    sems = refs[18]
-    loads = [pltpu.make_async_copy(refs[i], refs[12 + i], sems.at[0, i]) for i in range(6)]
-    stores = [pltpu.make_async_copy(refs[12 + i], refs[6 + i], sems.at[1, i]) for i in range(6)]
-    for copy in loads:
-        copy.start()
-    for copy, store in zip(loads, stores):
-        copy.wait()
+    sems = refs[12]
+    stores = [pltpu.make_async_copy(refs[i], refs[6 + i], sems.at[i]) for i in range(6)]
+    for store in stores:
         store.start()
     for store in stores:
         store.wait()
@@ -681,6 +663,7 @@
     rows = 1024
     smem = pl.BlockSpec(memory_space=pltpu.SMEM)
     hbm = pl.BlockSpec(memory_space=pltpu.HBM)
+    vmem = pl.BlockSpec(memory_space=pltpu.VMEM)
     shapes = [
         jax.ShapeDtypeStruct((rows, 128), BF16),
         jax.ShapeDtypeStruct((rows, 128), BF16),
@@ -691,9 +674,9 @@
     ]
     results = pl.pallas_call(
         functools.partial(kernel, scale),
-        out_shape=shapes,
+        out_shape=[pltpu.VMEM(s.shape, s.dtype) for s in shapes],
         in_specs=[smem] * 3 + [hbm] * 6,
-        out_specs=[hbm] * 6,
+        out_specs=[vmem] * 6,
         scratch_shapes=[
             *[pltpu.VMEM((2, 6, 64, 128), BF16)] * 32,
             *[pltpu.VMEM((8, 8, 64, 128), BF16)] * 4,
@@ -704,14 +687,11 @@
             pltpu.SMEM((80, 128), jnp.int32),
             pltpu.VMEM((64, 64, 128), F32),
             pltpu.VMEM((64, 128), jnp.int32),
-            pltpu.VMEM((1808, 128), F32),
             pltpu.VMEM((rows, 128), BF16),
             pltpu.VMEM((rows, 128), BF16),
             pltpu.VMEM((896, 128), BF16),
             pltpu.VMEM((896, 128), BF16),
             pltpu.VMEM((2, 1, 128), F32),
-            pltpu.VMEM((rows, 128), BF16),
-            pltpu.VMEM((rows, 128), BF16),
             pltpu.VMEM((1040, 128), F32),
             pltpu.VMEM((512, 128), F32),
             pltpu.VMEM((128, 128), F32),
@@ -741,7 +721,6 @@
             pltpu.SemaphoreType.DMA((4, 2)),
             pltpu.SemaphoreType.DMA((3, 2, 4)),
             pltpu.SemaphoreType.DMA((8,)),
-            pltpu.SemaphoreType.DMA((6,)),
         ],
         compiler_params=pltpu.CompilerParams(
             collective_id=0, has_side_effects=True, vmem_limit_bytes=56 * 1024 * 1024
@@ -760,13 +739,10 @@
     out, grad, w1, w2, g1, g2 = pl.pallas_call(
         hand_over,
         out_shape=shapes,
-        in_specs=[hbm] * 6,
+        in_specs=[vmem] * 6,
         out_specs=[hbm] * 6,
-        scratch_shapes=[
-            *[pltpu.VMEM(s.shape, s.dtype) for s in shapes],
-            pltpu.SemaphoreType.DMA((2, 6)),
-        ],
-    )(*results)
+        scratch_shapes=[pltpu.SemaphoreType.DMA((6,))],
+    )(*[pltpu.with_memory_space_constraint(r, pltpu.VMEM) for r in results])
     return (
         out.reshape(features.shape),
         grad.reshape(features.shape),

time: 91.4 us -> 89.6 us (0.980)
  Pallas kernels: 90.6 us -> 88.8 us
    pallas_call x2, Pallas kernels: 90.6 us -> 88.8 us  [the longest x1 87.7 us: shards(): pl.pallas_call(functools.partial(kernel, scale), out_shape=[pltpu.VMEM(s....]
where the time goes in v4:
time: 89.6 us; the launch traced here: 89.5 us
  Pallas kernels  88.8 us (99%)
    pallas_call x1, Pallas kernels, shards(): pl.pallas_call(functools.partial(kernel, scale), out_shape=[pltpu.VMEM(s....  87.7 us

profile of v4, /device:TPU:1, one launch (start us, length us, event | category | flops | bytes accessed | tf_op | source)
XLA Modules:
  0.0 89.5 jit_solution(753570165490131152)
XLA Ops:
  0.6 87.7 %shard_map.136 = (bf16[1024,128]{1,0:T(8,128)(2,1)S(1)}, bf16[1024,128]{1,0:T(8,128)(2,1)S(1)}, f32[896,128]{1,0:T(8,128)S(1)}, f32[896,128]{1,0:T(8,128)S(1)}, ...) custom-call(s32[64]{0:T(128)} %bitcast.20, s32[2,6]{1,0:T(2,128)} %bitcast.19, s32[2]{0:T(128)} %bitcast.21, ...), custom_call_target="tpu_custom_call" | custom-call | tf_op jit(solution)/shard_map/pallas_call | solution.py:675
  88.3 1.2 %shard_map.137 = (bf16[1024,128]{1,0:T(8,128)(2,1)}, bf16[1024,128]{1,0:T(8,128)(2,1)}, f32[896,128]{1,0:T(8,128)}, f32[896,128]{1,0:T(8,128)}, f32[1,128]{1,0:T(1,128)}, /*index=5*/f32[1,128]{1,0:T(1,128)}) custom-call(bf16[1024,128]{1,0:T(8,128)(2,1)S(1)} %get-tuple-element.18.refs_0_, bf16[1024,128]{1,0:T(8,128)(2,1)S(1)} %get-tuple-element.19.refs_1_, ...), custom_call_target="tpu_custom_call" | custom-call | tf_op jit(solution)/shard_map/pallas_call | solution.py:739

commit v5 on v4

--- a/solution.py
+++ b/solution.py
@@ -476,6 +476,7 @@
 
     lax.fori_loop(0, 12, halo_one, 0, unroll=UNH)
     add_faces(acc, lambda q: hal[q], w1_ref)
+    hop(1, 2)
 
     def hidden_rows(r):
         rows = pl.ds(r, 128)
@@ -485,7 +486,6 @@
 
     chunks(8, 128, hidden_rows)
     faces(2)
-    hop(1, 2)
     hop(2, 0)
 
     hop(1, 3)

time: 89.6 us -> 88.8 us (level)
  no operation moved by 1% of the time
where the time goes in v5:
time: 88.8 us; the launch traced here: 88.6 us
  Pallas kernels  88 us (99%)
    pallas_call x1, Pallas kernels, shards(): pl.pallas_call(functools.partial(kernel, scale), out_shape=[pltpu.VMEM(s....  86.9 us

profile of v5, /device:TPU:1, one launch (start us, length us, event | category | flops | bytes accessed | tf_op | source)
XLA Modules:
  0.0 88.6 jit_solution(1290228290952357889)
XLA Ops:
  0.6 86.9 %shard_map.136 = (bf16[1024,128]{1,0:T(8,128)(2,1)S(1)}, bf16[1024,128]{1,0:T(8,128)(2,1)S(1)}, f32[896,128]{1,0:T(8,128)S(1)}, f32[896,128]{1,0:T(8,128)S(1)}, ...) custom-call(s32[64]{0:T(128)} %bitcast.20, s32[2,6]{1,0:T(2,128)} %bitcast.19, s32[2]{0:T(128)} %bitcast.21, ...), custom_call_target="tpu_custom_call" | custom-call | tf_op jit(solution)/shard_map/pallas_call | solution.py:675
  87.5 1.2 %shard_map.137 = (bf16[1024,128]{1,0:T(8,128)(2,1)}, bf16[1024,128]{1,0:T(8,128)(2,1)}, f32[896,128]{1,0:T(8,128)}, f32[896,128]{1,0:T(8,128)}, f32[1,128]{1,0:T(1,128)}, /*index=5*/f32[1,128]{1,0:T(1,128)}) custom-call(bf16[1024,128]{1,0:T(8,128)(2,1)S(1)} %get-tuple-element.18.refs_0_, bf16[1024,128]{1,0:T(8,128)(2,1)S(1)} %get-tuple-element.19.refs_1_, ...), custom_call_target="tpu_custom_call" | custom-call | tf_op jit(solution)/shard_map/pallas_call | solution.py:739
